TPU v7x, 256 devices: a whole 4x4x8 slice. The times are simulated.
256 devices in a mesh: grp: 4 (over y_hi, core), uly: 8 (over z), ctx: 8 (over y_lo, x).
Axes of the slice: x: 4, y: 4 (y_hi: 2, y_lo: 2; y = y_hi * 2 + y_lo), z: 8, core: 2. Of those that a mesh axis runs over, the one named last changes fastest.
Arguments:
- queries: bfloat16 [32768, 4096], P(('grp', 'uly', 'ctx')), may hold values from -80 to 80
- keys_in: bfloat16 [32768, 1024], P(('grp', 'uly', 'ctx')), may hold values from -6 to 6
- values_in: bfloat16 [32768, 1024], P(('grp', 'uly', 'ctx')), may hold values from -6 to 6
- out_grad: bfloat16 [32768, 4096], P(('grp', 'uly', 'ctx')), may hold values from -6 to 6
- lengths: int32 [4, 2, 3], P('grp'), may hold values from 1 to 2048, 4096 in all within a row
- prompt_keys: bfloat16 [128, 1024], P(('grp', 'ctx'), 'uly'), may hold values from -6 to 6
- prompt_values: bfloat16 [128, 1024], P(('grp', 'ctx'), 'uly'), may hold values from -6 to 6
Outputs:
- attention_output: bfloat16 [32768, 4096], P(('grp', 'uly', 'ctx'))
- query_gradient: bfloat16 [32768, 4096], P(('grp', 'uly', 'ctx'))
- response_key_grad: bfloat16 [32768, 1024], P(('grp', 'uly', 'ctx'))
- response_value_grad: bfloat16 [32768, 1024], P(('grp', 'uly', 'ctx'))
- prompt_key_grad: bfloat16 [128, 1024], P(('grp', 'ctx'), 'uly')
- prompt_value_grad: bfloat16 [128, 1024], P(('grp', 'ctx'), 'uly')
All inputs are finite; a program needn't handle non-finite values.
Results may differ from a plain program's by a relative error of at most 0.03.
The roundings to bfloat16 on the way count: a program that leaves them out, or rounds other values in their place, can miss the bound.
Values may be sent and summed in bfloat16 or wider, within the bound.
A program may use at most 128 MiB of HBM per device.

v0:
```python
import jax
import jax.numpy as jnp
from jax import lax
from jax.sharding import PartitionSpec as P

H = 32
KEY_VALUE_HEADS = 8
HEAD_WIDTH = 128
PROMPT_TOKENS = 128


theta_base = 1000000.0
neg_fill = -1e30


def rotate_rows(values, positions, direction):
    count = values.shape[0]
    half_dim = HEAD_WIDTH // 2
    shaped = values.astype(jnp.float32).reshape(count, -1, HEAD_WIDTH)
    frequency = jnp.exp(
        -(2.0 * jnp.arange(half_dim, dtype=jnp.float32) / HEAD_WIDTH)
        * jnp.log(jnp.float32(theta_base))
    )
    angles = positions.astype(jnp.float32)[:, None] * frequency[None, :]
    cosine = jnp.cos(angles)[:, None, :]
    sine_part = direction * jnp.sin(angles)[:, None, :]
    first_half = shaped[..., :half_dim]
    second_half = shaped[..., half_dim:]
    turned = jnp.concatenate(
        [
            first_half * cosine - second_half * sine_part,
            second_half * cosine + first_half * sine_part,
        ],
        axis=-1,
    )
    return turned.reshape(count, -1)


def segment_begins(length_row, count):
    segment_ends = jnp.cumsum(length_row)
    token_index = jnp.arange(count, dtype=jnp.int32)
    closed = (segment_ends[None, :] <= token_index[:, None]).astype(jnp.int32)
    return jnp.sum(length_row[None, :] * closed, axis=1)


def group_begins(length_rows, run_len):
    run_count = length_rows.shape[0]
    starts = jax.vmap(lambda row: segment_begins(row, run_len))(length_rows)
    offsets = (jnp.arange(run_count, dtype=jnp.int32) * run_len)[:, None]
    return (starts + offsets).reshape(-1)


def attend_block(query_blk, grad_blk, keys_win, values_win, prompt_k, prompt_v, allowed):
    score_scale = HEAD_WIDTH ** (-0.5)
    key_block = jnp.concatenate([prompt_k, keys_win], axis=0)
    value_block = jnp.concatenate([prompt_v, values_win], axis=0)
    scores = (
        jnp.einsum("qhgd,khd->hgqk", query_blk, key_block, preferred_element_type=jnp.float32)
        * score_scale
    )
    live_mask = jnp.concatenate(
        [jnp.ones((allowed.shape[0], prompt_k.shape[0]), dtype=bool), allowed], axis=1
    )
    scores = jnp.where(live_mask[None, None], scores, neg_fill)
    row_top = jnp.max(scores, axis=-1, keepdims=True)
    powered = jnp.exp(scores - row_top)
    attn_prob = powered / jnp.sum(powered, axis=-1, keepdims=True)
    prob_half = attn_prob.astype(jnp.bfloat16)
    output_halfway = jnp.einsum(
        "hgqk,khd->qhgd", prob_half, value_block, preferred_element_type=jnp.float32
    ).astype(jnp.bfloat16)
    row_delta = jnp.sum(grad_blk.astype(jnp.float32) * output_halfway.astype(jnp.float32), axis=-1)
    prob_grad = jnp.einsum(
        "qhgd,khd->hgqk", grad_blk, value_block, preferred_element_type=jnp.float32
    )
    score_grad = (
        attn_prob * (prob_grad - jnp.transpose(row_delta, (1, 2, 0))[..., None]) * score_scale
    ).astype(jnp.bfloat16)
    query_piece = jnp.einsum(
        "hgqk,khd->qhgd", score_grad, key_block, preferred_element_type=jnp.float32
    )
    key_part = jnp.einsum(
        "hgqk,qhgd->khd", score_grad, query_blk, preferred_element_type=jnp.float32
    )
    value_part = jnp.einsum(
        "hgqk,qhgd->khd", prob_half, grad_blk, preferred_element_type=jnp.float32
    )
    prompt_length = prompt_k.shape[0]
    return (
        output_halfway,
        query_piece,
        key_part[:prompt_length],
        key_part[prompt_length:],
        value_part[:prompt_length],
        value_part[prompt_length:],
    )


def local(queries, keys_in, values_in, out_grad, lengths, prompt_keys, prompt_values):
    uly_count = lax.axis_size("uly")
    ctx_count = lax.axis_size("ctx")
    block_len = queries.shape[0]
    group_tokens = block_len * ctx_count * uly_count
    run_count = lengths.shape[1]
    run_len = group_tokens // run_count
    window = run_len // 2 + block_len
    local_kv = KEY_VALUE_HEADS // uly_count
    group_size = H // KEY_VALUE_HEADS
    ctx_place = lax.axis_index("ctx")
    begins = group_begins(lengths[0], run_len)
    all_positions = PROMPT_TOKENS + jnp.arange(group_tokens, dtype=jnp.int32) - begins
    own_tokens = (
        (jnp.arange(uly_count, dtype=jnp.int32)[:, None] * ctx_count + ctx_place) * block_len
        + jnp.arange(block_len, dtype=jnp.int32)[None, :]
    ).reshape(-1)
    own_positions = jnp.take(all_positions, own_tokens)
    home_tokens = (lax.axis_index("uly") * ctx_count + ctx_place) * block_len + jnp.arange(
        block_len, dtype=jnp.int32
    )
    home_positions = jnp.take(all_positions, home_tokens)
    query_x, grad_x = (
        lax.all_to_all(queries, "uly", split_axis=1, concat_axis=0, tiled=True),
        lax.all_to_all(out_grad, "uly", split_axis=1, concat_axis=0, tiled=True),
    )
    key_home = rotate_rows(keys_in, home_positions, 1.0).astype(jnp.bfloat16)
    key_wide, value_wide = (
        lax.all_gather(key_home, "ctx", axis=0, tiled=True),
        lax.all_gather(values_in, "ctx", axis=0, tiled=True),
    )
    keys_glob, values_glob = (
        lax.all_to_all(key_wide, "uly", split_axis=1, concat_axis=0, tiled=True),
        lax.all_to_all(value_wide, "uly", split_axis=1, concat_axis=0, tiled=True),
    )
    prompt_k, prompt_v = (
        lax.all_gather(prompt_keys, ("grp", "ctx"), axis=0, tiled=True),
        lax.all_gather(prompt_values, ("grp", "ctx"), axis=0, tiled=True),
    )
    prompt_length = prompt_k.shape[0]
    prompt_k3 = prompt_k.reshape(prompt_length, local_kv, HEAD_WIDTH)
    prompt_v3 = prompt_v.reshape(prompt_length, local_kv, HEAD_WIDTH)
    key_three = keys_glob.reshape(group_tokens, local_kv, HEAD_WIDTH)
    value_three = values_glob.reshape(group_tokens, local_kv, HEAD_WIDTH)
    query_rot = rotate_rows(query_x, own_positions, 1.0).astype(jnp.bfloat16)
    query_blocks = query_rot.reshape(uly_count, block_len, local_kv, group_size, HEAD_WIDTH)
    grad_blocks = grad_x.reshape(uly_count, block_len, local_kv, group_size, HEAD_WIDTH)

    def step_block(carried_state, item):
        key_running_sum, value_running_sum, prompt_key_running, prompt_value_running = carried_state
        block_id, query_blk, grad_blk = item
        query_start = (block_id * ctx_count + ctx_place) * block_len
        window_start = jnp.maximum(query_start + block_len - window, 0)
        keys_win = lax.dynamic_slice_in_dim(key_three, window_start, window, 0)
        values_win = lax.dynamic_slice_in_dim(value_three, window_start, window, 0)
        query_pos = query_start + jnp.arange(block_len, dtype=jnp.int32)
        key_pos = window_start + jnp.arange(window, dtype=jnp.int32)
        begins_blk = lax.dynamic_slice_in_dim(begins, query_start, block_len, 0)
        allowed = (key_pos[None, :] >= begins_blk[:, None]) & (
            key_pos[None, :] <= query_pos[:, None]
        )
        output_halfway, query_piece, prompt_key_piece, key_part, prompt_value_piece, value_part = (
            attend_block(query_blk, grad_blk, keys_win, values_win, prompt_k3, prompt_v3, allowed)
        )
        key_running_sum = lax.dynamic_update_slice_in_dim(
            key_running_sum,
            lax.dynamic_slice_in_dim(key_running_sum, window_start, window, 0) + key_part,
            window_start,
            0,
        )
        value_running_sum = lax.dynamic_update_slice_in_dim(
            value_running_sum,
            lax.dynamic_slice_in_dim(value_running_sum, window_start, window, 0) + value_part,
            window_start,
            0,
        )
        return (
            (
                key_running_sum,
                value_running_sum,
                prompt_key_running + prompt_key_piece,
                prompt_value_running + prompt_value_piece,
            ),
            (output_halfway, query_piece),
        )

    start_state = (
        jnp.zeros((group_tokens, local_kv, HEAD_WIDTH), jnp.float32),
        jnp.zeros((group_tokens, local_kv, HEAD_WIDTH), jnp.float32),
        jnp.zeros((prompt_length, local_kv, HEAD_WIDTH), jnp.float32),
        jnp.zeros((prompt_length, local_kv, HEAD_WIDTH), jnp.float32),
    )
    closing_state, stacked = lax.scan(
        step_block, start_state, (jnp.arange(uly_count, dtype=jnp.int32), query_blocks, grad_blocks)
    )
    key_running_sum, value_running_sum, prompt_key_running, prompt_value_running = closing_state
    output_halfway, query_piece = stacked
    local_rows = uly_count * block_len
    output_rows = output_halfway.reshape(local_rows, -1)
    query_back = rotate_rows(query_piece.reshape(local_rows, -1), own_positions, -1.0).astype(
        jnp.bfloat16
    )
    key_parts, value_parts = (
        lax.all_to_all(
            key_running_sum.reshape(group_tokens, -1).astype(jnp.bfloat16),
            "uly",
            split_axis=0,
            concat_axis=1,
            tiled=True,
        ).astype(jnp.float32),
        lax.all_to_all(
            value_running_sum.reshape(group_tokens, -1).astype(jnp.bfloat16),
            "uly",
            split_axis=0,
            concat_axis=1,
            tiled=True,
        ).astype(jnp.float32),
    )
    key_sum, value_sum = (
        lax.psum_scatter(
            key_parts.astype(jnp.bfloat16), "ctx", scatter_dimension=0, tiled=True
        ).astype(jnp.float32),
        lax.psum_scatter(
            value_parts.astype(jnp.bfloat16), "ctx", scatter_dimension=0, tiled=True
        ).astype(jnp.float32),
    )
    response_key_grad = rotate_rows(key_sum, home_positions, -1.0).astype(jnp.bfloat16)
    response_value_grad = value_sum.astype(jnp.bfloat16)
    attention_output, query_gradient = (
        lax.all_to_all(output_rows, "uly", split_axis=0, concat_axis=1, tiled=True),
        lax.all_to_all(query_back, "uly", split_axis=0, concat_axis=1, tiled=True),
    )
    prompt_kterm = prompt_key_running.reshape(prompt_length, -1)
    prompt_value_addend = prompt_value_running.reshape(prompt_length, -1)
    prompt_ksum, prompt_vsum = (
        lax.psum_scatter(
            prompt_kterm.astype(jnp.bfloat16), ("grp", "ctx"), scatter_dimension=0, tiled=True
        ).astype(jnp.float32),
        lax.psum_scatter(
            prompt_value_addend.astype(jnp.bfloat16),
            ("grp", "ctx"),
            scatter_dimension=0,
            tiled=True,
        ).astype(jnp.float32),
    )
    return (
        attention_output,
        query_gradient,
        response_key_grad,
        response_value_grad,
        prompt_ksum.astype(jnp.bfloat16),
        prompt_vsum.astype(jnp.bfloat16),
    )


def solution(mesh):
    in_specs = (
        P(("grp", "uly", "ctx"), None),
        P(("grp", "uly", "ctx"), None),
        P(("grp", "uly", "ctx"), None),
        P(("grp", "uly", "ctx"), None),
        P("grp", None, None),
        P(("grp", "ctx"), "uly"),
        P(("grp", "ctx"), "uly"),
    )
    out_specs = (
        P(("grp", "uly", "ctx"), None),
        P(("grp", "uly", "ctx"), None),
        P(("grp", "uly", "ctx"), None),
        P(("grp", "uly", "ctx"), None),
        P(("grp", "ctx"), "uly"),
        P(("grp", "ctx"), "uly"),
    )
    return jax.shard_map(local, mesh=mesh, in_specs=in_specs, out_specs=out_specs, check_vma=False)
```

profile of v0, /device:TPU:64, one launch (start us, length us, event | category | flops | bytes accessed | tf_op | source)
XLA Modules:
  0.0 864.0 jit_solution(2329381717888470953)
XLA Ops:
  14.5 8.2 all-to-all-start
  24.1 25.0 %all-to-all-done = bf16[128,8,512]{0,2,1:T(8,128)(2,1)S(1)} async-done(((bf16[128,8,512]{0,2,1:T(8,128)(2,1)}), bf16[128,8,512]{0,2,1:T(8,128)(2,1)S(1)}, u32[]{:S(2)}, u32[]{:S(2)}) %all-to-all-start) | async-done | bytes 1048608 | tf_op jit(solution)/shard_map/all_to_all | solution.py:122
  49.1 6.6 all-to-all-start.3
  56.4 26.2 %all-to-all-done.3 = bf16[128,8,512]{0,2,1:T(8,128)(2,1)} async-done(((bf16[128,8,512]{0,2,1:T(8,128)(2,1)}), bf16[128,8,512]{0,2,1:T(8,128)(2,1)}, u32[]{:S(2)}, u32[]{:S(2)}) %all-to-all-start.3) | async-done | bytes 1048608 | tf_op jit(solution)/shard_map/all_to_all | solution.py:123
  88.5 21.7 %all-gather.7.cloned.1.call-done = bf16[1024,1024]{1,0:T(8,128)(2,1)} async-done(((bf16[128,1024]{1,0:T(8,128)(2,1)}), bf16[1024,1024]{1,0:T(8,128)(2,1)}) %all-gather.7.cloned.1.call-update) | async-done | bytes 2097168 | tf_op jit(solution)/shard_map/all_gather | solution.py:128
  113.5 24.4 %all-to-all-done.1 = bf16[1024,8,128]{0,2,1:T(8,128)(2,1)S(1)} async-done(((bf16[1024,8,128]{0,2,1:T(8,128)(2,1)}), bf16[1024,8,128]{0,2,1:T(8,128)(2,1)S(1)}, u32[]{:S(2)}, u32[]{:S(2)}) %all-to-all-start.1) | async-done | bytes 2097184 | tf_op jit(solution)/shard_map/all_to_all | solution.py:131
  142.4 6.2 gather_fusion
  148.6 66.5 %all-gather = bf16[32,4,128]{2,1,0:T(4,128)(2,1)S(1)} all-gather(bf16[1,4,128]{2,1,0:T(4,128)(2,1)S(1)} %bitcast.241), channel_id=1, replica_groups=mesh['grp'=4,'uly'=8,'ctx'=8] {'grp','ctx'}, dimensions={0}, use_global_device_ids=true | all-gather | bytes 33792 | tf_op jit(solution)/shard_map/all_gather | solution.py:135
  215.1 61.2 %all-gather.1 = bf16[32,4,128]{2,1,0:T(4,128)(2,1)S(1)} all-gather(bf16[1,4,128]{2,1,0:T(4,128)(2,1)S(1)} %bitcast.242), channel_id=1, replica_groups=mesh['grp'=4,'uly'=8,'ctx'=8] {'grp','ctx'}, dimensions={0}, use_global_device_ids=true | all-gather | bytes 33792 | tf_op jit(solution)/shard_map/all_gather | solution.py:136
  292.2 352.7 %while.25 = (s32[]{:T(128)}, f32[8192,1,128]{2,0,1:T(8,128)}, f32[8192,1,128]{0,2,1:T(8,128)}, f32[128,1,128]{0,2,1:T(8,128)}, f32[128,1,128]{0,2,1:T(8,128)}, /...) while((s32[]{:T(128)}, f32[8192,1,128]{2,0,1:T(8,128)}, ...), condition=%wide.region_6.7_spmd.clone, body=%wide.region_2.0_spmd.clone.sunk | while | flops 1834959616 | bytes 72230040 | solution.py:191
  328.0 6.2 dynamic_update_slice.51
  372.2 6.2 dynamic_update_slice.51
  416.3 6.2 dynamic_update_slice.51
  460.5 6.2 dynamic_update_slice.51
  504.6 6.2 dynamic_update_slice.51
  548.8 6.2 dynamic_update_slice.51
  648.7 6.1 all-to-all-start.6
  656.3 39.7 %all-to-all-done.6 = bf16[8,1024,128]{2,1,0:T(8,128)(2,1)S(1)} async-done(((bf16[8,1024,128]{2,1,0:T(8,128)(2,1)}), bf16[8,1024,128]{2,1,0:T(8,128)(2,1)S(1)}, u32[]{:S(2)}, u32[]{:S(2)}) %all-to-all-start.6) | async-done | bytes 2097184 | tf_op jit(solution)/shard_map/all_to_all | solution.py:202
  707.5 7.0 all-to-all-start.7
  721.1 36.3 %all-to-all-done.7 = bf16[8,1024,128]{2,1,0:T(8,128)(2,1)} async-done(((bf16[8,1024,128]{2,1,0:T(8,128)(2,1)}), bf16[8,1024,128]{2,1,0:T(8,128)(2,1)}, u32[]{:S(2)}, u32[]{:S(2)}) %all-to-all-start.7) | async-done | bytes 2097184 | tf_op jit(solution)/shard_map/all_to_all | solution.py:209
  773.2 20.2 %all-to-all-done.5 = bf16[8,128,512]{1,2,0:T(8,128)(2,1)S(1)} async-done(((bf16[8,128,512]{1,2,0:T(8,128)(2,1)}), bf16[8,128,512]{1,2,0:T(8,128)(2,1)S(1)}, u32[]{:S(2)}, u32[]{:S(2)}) %all-to-all-start.5) | async-done | bytes 1048608 | tf_op jit(solution)/shard_map/all_to_all | solution.py:229
  793.5 7.2 all-to-all-start.4
  804.5 17.8 %all-to-all-done.4 = bf16[8,128,512]{2,1,0:T(8,128)(2,1)S(1)} async-done(((bf16[8,128,512]{2,1,0:T(8,128)(2,1)}), bf16[8,128,512]{2,1,0:T(8,128)(2,1)S(1)}, u32[]{:S(2)}, u32[]{:S(2)}) %all-to-all-start.4) | async-done | bytes 1048608 | tf_op jit(solution)/shard_map/all_to_all | solution.py:228
  826.5 31.0 %reduce-scatter.9.cloned.1.call-done = bf16[128,1024]{1,0:T(8,128)(2,1)} async-done(((bf16[1024,1024]{1,0:T(8,128)(2,1)}), bf16[128,1024]{1,0:T(8,128)(2,1)}) %reduce-scatter.9.cloned.1.call-update) | async-done | bytes 262160
  (494 shorter events, 394.3 us)
Async XLA Ops:
  7.2 75.4 %all-gather.5.cloned.1.call-start = ((), (), s32[]{:S(2)}) async-start(), calls=%async_computation.10 | async-start | bytes 2359296 | tf_op jit(solution)/shard_map/all_gather | solution.py:127
  14.5 8.3 copy-start.20
  14.5 34.5 %all-to-all-start = ((bf16[128,8,512]{0,2,1:T(8,128)(2,1)}), bf16[128,8,512]{0,2,1:T(8,128)(2,1)S(1)}, u32[]{:S(2)}, u32[]{:S(2)}) async-start(bf16[128,8,512]{0,2,1:T(8,128)(2,1)} %bitcast), calls=%async_computation | async-start | bytes 2097152 | tf_op jit(solution)/shard_map/all_to_all | solution.py:122
  49.1 33.5 %all-to-all-start.3 = ((bf16[128,8,512]{0,2,1:T(8,128)(2,1)}), bf16[128,8,512]{0,2,1:T(8,128)(2,1)}, u32[]{:S(2)}, u32[]{:S(2)}) async-start(bf16[128,8,512]{0,2,1:T(8,128)(2,1)} %bitcast.18), calls=%async_computation.3 | async-start | bytes 2097152 | tf_op jit(solution)/shard_map/all_to_all | solution.py:123
  55.6 54.5 %all-gather.7.cloned.1.call-start = ((), (), s32[]{:S(2)}) async-start(), calls=%async_computation.11 | async-start | bytes 2359296 | tf_op jit(solution)/shard_map/all_gather | solution.py:128
  82.5 55.4 %all-to-all-start.1 = ((bf16[1024,8,128]{0,2,1:T(8,128)(2,1)}), bf16[1024,8,128]{0,2,1:T(8,128)(2,1)S(1)}, u32[]{:S(2)}, u32[]{:S(2)}) async-start(bf16[1024,8,128]{0,2,1:T(8,128)(2,1)} %bitcast.224), calls=%async_computation.1 | async-start | bytes 4194304 | tf_op jit(solution)/shard_map/all_to_all | solution.py:131
  137.9 149.6 %all-to-all-start.2 = ((bf16[1024,8,128]{2,0,1:T(8,128)(2,1)}), bf16[1024,8,128]{2,0,1:T(8,128)(2,1)}, u32[]{:S(2)}, u32[]{:S(2)}) async-start(bf16[1024,8,128]{2,0,1:T(8,128)(2,1)} %copy_bitcast_fusion), calls=%async_computation.2 | async-start | bytes 4194304 | tf_op jit(solution)/shard_map/all_to_all | solution.py:132
  142.4 72.7 %copy-start.28 = (bf16[4,128]{1,0:T(4,128)(2,1)S(1)}, bf16[4,128]{1,0:T(4,128)(2,1)}, u32[]{:S(2)}) copy-start(bf16[4,128]{1,0:T(4,128)(2,1)} %param.15) | copy-start | bytes 3076
  292.2 10.2 %copy-start.15 = (bf16[128,1,128]{2,0,1:T(8,128)(2,1)}, bf16[128,1,128]{2,0,1:T(8,128)(2,1)S(1)}, u32[]{:S(2)}) copy-start(bf16[128,1,128]{2,0,1:T(8,128)(2,1)S(1)} %get-tuple-element.733) | copy-start | bytes 98308 | tf_op jit(solution)/shard_map/while
  336.3 10.2 %copy-start.15 = (bf16[128,1,128]{2,0,1:T(8,128)(2,1)}, bf16[128,1,128]{2,0,1:T(8,128)(2,1)S(1)}, u32[]{:S(2)}) copy-start(bf16[128,1,128]{2,0,1:T(8,128)(2,1)S(1)} %get-tuple-element.733) | copy-start | bytes 98308 | tf_op jit(solution)/shard_map/while
  380.5 10.2 %copy-start.15 = (bf16[128,1,128]{2,0,1:T(8,128)(2,1)}, bf16[128,1,128]{2,0,1:T(8,128)(2,1)S(1)}, u32[]{:S(2)}) copy-start(bf16[128,1,128]{2,0,1:T(8,128)(2,1)S(1)} %get-tuple-element.733) | copy-start | bytes 98308 | tf_op jit(solution)/shard_map/while
  424.6 10.2 %copy-start.15 = (bf16[128,1,128]{2,0,1:T(8,128)(2,1)}, bf16[128,1,128]{2,0,1:T(8,128)(2,1)S(1)}, u32[]{:S(2)}) copy-start(bf16[128,1,128]{2,0,1:T(8,128)(2,1)S(1)} %get-tuple-element.733) | copy-start | bytes 98308 | tf_op jit(solution)/shard_map/while
  468.7 10.2 %copy-start.15 = (bf16[128,1,128]{2,0,1:T(8,128)(2,1)}, bf16[128,1,128]{2,0,1:T(8,128)(2,1)S(1)}, u32[]{:S(2)}) copy-start(bf16[128,1,128]{2,0,1:T(8,128)(2,1)S(1)} %get-tuple-element.733) | copy-start | bytes 98308 | tf_op jit(solution)/shard_map/while
  512.9 10.2 %copy-start.15 = (bf16[128,1,128]{2,0,1:T(8,128)(2,1)}, bf16[128,1,128]{2,0,1:T(8,128)(2,1)S(1)}, u32[]{:S(2)}) copy-start(bf16[128,1,128]{2,0,1:T(8,128)(2,1)S(1)} %get-tuple-element.733) | copy-start | bytes 98308 | tf_op jit(solution)/shard_map/while
  557.0 10.2 %copy-start.15 = (bf16[128,1,128]{2,0,1:T(8,128)(2,1)}, bf16[128,1,128]{2,0,1:T(8,128)(2,1)S(1)}, u32[]{:S(2)}) copy-start(bf16[128,1,128]{2,0,1:T(8,128)(2,1)S(1)} %get-tuple-element.733) | copy-start | bytes 98308 | tf_op jit(solution)/shard_map/while
  601.1 10.2 %copy-start.15 = (bf16[128,1,128]{2,0,1:T(8,128)(2,1)}, bf16[128,1,128]{2,0,1:T(8,128)(2,1)S(1)}, u32[]{:S(2)}) copy-start(bf16[128,1,128]{2,0,1:T(8,128)(2,1)S(1)} %get-tuple-element.733) | copy-start | bytes 98308 | tf_op jit(solution)/shard_map/while
  648.7 47.3 %all-to-all-start.6 = ((bf16[8,1024,128]{2,1,0:T(8,128)(2,1)}), bf16[8,1024,128]{2,1,0:T(8,128)(2,1)S(1)}, u32[]{:S(2)}, u32[]{:S(2)}) async-start(bf16[8,1024,128]{2,1,0:T(8,128)(2,1)} %bitcast.27), calls=%async_computation.6 | async-start | bytes 4194304 | tf_op jit(solution)/shard_map/all_to_all | solution.py:202
  654.8 147.1 %all-reduce.6.cloned.1.call-start = ((), (), s32[]{:S(2)}) async-start(), calls=%async_computation.14 | async-start | bytes 131072
  656.2 168.1 %reduce-scatter.7.cloned.1.call-start = ((), (), s32[]{:S(2)}) async-start(), calls=%async_computation.12 | async-start | bytes 2359296
  707.5 49.9 %all-to-all-start.7 = ((bf16[8,1024,128]{2,1,0:T(8,128)(2,1)}), bf16[8,1024,128]{2,1,0:T(8,128)(2,1)}, u32[]{:S(2)}, u32[]{:S(2)}) async-start(bf16[8,1024,128]{2,1,0:T(8,128)(2,1)} %bitcast.217), calls=%async_computation.7 | async-start | bytes 4194304 | tf_op jit(solution)/shard_map/all_to_all | solution.py:209
  714.5 143.0 %reduce-scatter.9.cloned.1.call-start = ((), (), s32[]{:S(2)}) async-start(), calls=%async_computation.13 | async-start | bytes 2359296
  766.0 27.4 %all-to-all-start.5 = ((bf16[8,128,512]{1,2,0:T(8,128)(2,1)}), bf16[8,128,512]{1,2,0:T(8,128)(2,1)S(1)}, u32[]{:S(2)}, u32[]{:S(2)}) async-start(bf16[8,128,512]{1,2,0:T(8,128)(2,1)} %copy.204), calls=%async_computation.5 | async-start | bytes 2097152 | tf_op jit(solution)/shard_map/all_to_all | solution.py:229
  771.9 28.7 %copy-start.29 = (u32[256]{0:T(256)S(1)}, u32[256]{0:T(256)}, u32[]{:S(2)}) copy-start(u32[256]{0:T(256)} %constant.180) | copy-start | bytes 3076
  793.5 28.8 %all-to-all-start.4 = ((bf16[8,128,512]{2,1,0:T(8,128)(2,1)}), bf16[8,128,512]{2,1,0:T(8,128)(2,1)S(1)}, u32[]{:S(2)}, u32[]{:S(2)}) async-start(bf16[8,128,512]{2,1,0:T(8,128)(2,1)} %copy.224), calls=%async_computation.4 | async-start | bytes 2097152 | tf_op jit(solution)/shard_map/all_to_all | solution.py:228
  (89 other events, 366.3 us)
Sparse Core Ops, SparseCore 0:
  13.3 49.1 all-gather.4
  64.3 45.7 all-gather.6
  659.0 104.8 all-reduce.5
  766.5 43.7 reduce-scatter.6
  813.4 44.0 reduce-scatter.8
where the time goes:
time: 871 us; the launch traced here: 864 us
  local copies, waits for them, and re-layouts  245 us (28%)
  waiting for transfers between devices  243 us (28%)
  blocking collectives  128 us (15%)
  matrix products  90.9 us (10%)
  other arithmetic  84.3 us (10%)
  starting transfers between devices  51.4 us (6%)
  between operations  14.8 us (2%)
    all_gather x1, blocking collectives, local(): lax.all_gather(prompt_keys, ('grp', 'ctx'), axis=0, tiled=True)  66.5 us
    all_gather x1, blocking collectives, local(): lax.all_gather(prompt_values, ('grp', 'ctx'), axis=0, tiled=True)  61.2 us
    dynamic_update_slice x16, local copies, waits for them, and re-layouts, step_block(): lax.dynamic_update_slice_in_dim(key_running_sum, lax.dynamic_slice_in_dim...  56.6 us
    dynamic_update_slice x8, local copies, waits for them, and re-layouts, step_block(): lax.dynamic_update_slice_in_dim(value_running_sum, lax.dynamic_slice_in_d...  49.1 us
    dynamic_slice x16, local copies, waits for them, and re-layouts, step_block(): lax.dynamic_slice_in_dim(key_running_sum, window_start, window, 0)  40 us
    all_to_all x1, waiting for transfers between devices, local(): lax.all_to_all(key_running_sum.reshape(group_tokens, -1).astype(jnp.bfloa...  39.7 us
    all_to_all x1, waiting for transfers between devices, local(): lax.all_to_all(value_running_sum.reshape(group_tokens, -1).astype(jnp.bfl...  36.3 us
    unnamed x8, waiting for transfers between devices  31.8 us
  transfers between devices with their start and end apart: 13, of which 9 were waited for; matrix products, arithmetic and copies ran while one was open for 7% of the time, Pallas kernels for 0%

commit v1 on v0

v1 whole, which is shorter than its diff:
```python
import functools

import jax
import jax.numpy as jnp
import numpy as np
from jax import lax
from jax.experimental import pallas as pl
from jax.experimental.pallas import tpu as pltpu
from jax.sharding import PartitionSpec as P

H = 32
KEY_VALUE_HEADS = 8
HEAD_WIDTH = 128
PROMPT_TOKENS = 128
theta_base = 1000000.0
neg_fill = -1e30

N_GRP, N_ULY, N_CTX = 4, 8, 8
BLOCK = 128
CHUNK = N_CTX * BLOCK
RUN_PLACES = 4
RESP = 3
QH = H // KEY_VALUE_HEADS
WIN = 3 * CHUNK
TK = 256
TQ = 256
LANES = QH * TQ
SCALE = HEAD_WIDTH**-0.5
C2 = SCALE * 1.4426950408889634
MESH = pl.DeviceIdType.MESH
f32, bf16 = jnp.float32, jnp.bfloat16


def frequencies():
    half = np.exp(-(2.0 * np.arange(64) / HEAD_WIDTH) * np.log(theta_base)).astype(np.float32)
    return np.concatenate([half, half])


def begins_of(tau, len_ref, run):
    l0, l1 = len_ref[run, 0], len_ref[run, 1]
    l2 = len_ref[run, 2]
    e1 = l0 + l1
    zero = jnp.zeros_like(tau)
    return (
        jnp.where(tau >= l0, l0, zero)
        + jnp.where(tau >= e1, l1, zero)
        + jnp.where(tau >= e1 + l2, l2, zero)
    )


def cos_sin(base, freq_ref, len_ref, run):
    tau = base + lax.broadcasted_iota(jnp.int32, (BLOCK, HEAD_WIDTH), 0)
    pos = PROMPT_TOKENS + tau - begins_of(tau, len_ref, run)
    angle = pos.astype(f32) * freq_ref[0:1, :]
    lane = lax.broadcasted_iota(jnp.int32, (BLOCK, HEAD_WIDTH), 1)
    sine = jnp.sin(angle)
    return jnp.cos(angle), jnp.where(lane < 64, -sine, sine)


def send_in(
    q_ref, do_ref, k_ref, v_ref, len_ref, pk_ref, pv_ref, freq_ref,
    qx, dox, kvw, pt,
    qrot, kvs, ptile,
    q_s, q_r, d_s, d_r, kv_s, kv_r, f_s, f_r, g_s, g_r, p_s, p_r, loc,
):
    g, z, c = lax.axis_index("grp"), lax.axis_index("uly"), lax.axis_index("ctx")
    zr = lax.rem(z, RUN_PLACES)
    run = z // RUN_PLACES
    has_next, has_prev = zr < RUN_PLACES - 1, zr > 0
    relays = (zr == 1) | (zr == 2)
    gets_far = zr >= 2
    is_diag = z == c
    barrier = pltpu.get_barrier_semaphore()

    def greet(k, _):
        pl.semaphore_signal(barrier, inc=1, device_id=(g, z, lax.rem(c + k, N_CTX)), device_id_type=MESH)
        return 0

    lax.fori_loop(1, N_CTX, greet, 0)

    @pl.when(has_prev)
    def _():
        pl.semaphore_signal(barrier, inc=1, device_id=(g, z - 1, c), device_id_type=MESH)

    def greet_prompt(n, _):
        gg, cc = n // N_CTX, lax.rem(n, N_CTX)

        @pl.when(jnp.logical_not(is_diag & (gg == g) & (cc == c)))
        def _():
            pl.semaphore_signal(barrier, inc=1, device_id=(gg, c, cc), device_id_type=MESH)

        return 0

    lax.fori_loop(0, N_GRP * N_CTX, greet_prompt, 0)

    cosine, sine = cos_sin(zr * CHUNK + c * BLOCK, freq_ref, len_ref, run)

    def turned(block):
        x = block.astype(f32)
        return (x * cosine + pltpu.roll(x, 64, 1) * sine).astype(bf16)

    for j in range(KEY_VALUE_HEADS):
        kvs[:, 256 * j : 256 * j + 128] = turned(k_ref[:, 128 * j : 128 * j + 128])
        kvs[:, 256 * j + 128 : 256 * j + 256] = v_ref[:, 128 * j : 128 * j + 128]
    ptile[0:4, :] = pk_ref[...].astype(f32)
    ptile[4:8, :] = pv_ref[...].astype(f32)

    targets = (
        (N_CTX - 1)
        + jnp.where(has_next, 1, 0)
        + N_GRP * N_ULY
        - jnp.where(is_diag, 1, 0)
    )
    pl.semaphore_wait(barrier, targets)

    def remote(src, dst, s, r, dev):
        return pltpu.make_async_remote_copy(
            src_ref=src, dst_ref=dst, send_sem=s, recv_sem=r, device_id=dev, device_id_type=MESH
        )

    def rows(at):
        return pl.ds(pl.multiple_of(at, BLOCK), BLOCK)

    def kv_copy(peer):
        return remote(
            kvs.at[:, pl.ds(pl.multiple_of(peer * 256, 256), 256)],
            kvw.at[rows(2 * CHUNK + c * BLOCK), :],
            kv_s.at[peer], kv_r.at[c], (g, z, peer),
        )

    def kv_arrival(j):
        return remote(
            kvs.at[:, pl.ds(0, 256)], kvw.at[rows(2 * CHUNK + j * BLOCK), :],
            kv_s.at[j], kv_r.at[j], (g, z, j),
        )

    def d_copy(peer):
        return remote(
            do_ref.at[:, pl.ds(pl.multiple_of(peer * 512, 512), 512)],
            dox.at[rows(c * BLOCK), :], d_s.at[peer], d_r.at[c], (g, z, peer),
        )

    def d_arrival(j):
        return remote(
            do_ref.at[:, pl.ds(0, 512)], dox.at[rows(j * BLOCK), :], d_s.at[j], d_r.at[j], (g, z, j)
        )

    def q_copy(peer):
        return remote(
            qrot.at[:, pl.ds(pl.multiple_of(peer * 512, 512), 512)],
            qx.at[rows(c * BLOCK), :], q_s.at[peer], q_r.at[c], (g, z, peer),
        )

    def q_arrival(j):
        return remote(
            qrot.at[:, pl.ds(0, 512)], qx.at[rows(j * BLOCK), :], q_s.at[j], q_r.at[j], (g, z, j)
        )

    def own_copies():
        return (
            pltpu.make_async_copy(
                kvs.at[:, pl.ds(pl.multiple_of(c * 256, 256), 256)],
                kvw.at[rows(2 * CHUNK + c * BLOCK), :], loc.at[0],
            ),
            pltpu.make_async_copy(
                do_ref.at[:, pl.ds(pl.multiple_of(c * 512, 512), 512)],
                dox.at[rows(c * BLOCK), :], loc.at[1],
            ),
            pltpu.make_async_copy(
                qrot.at[:, pl.ds(pl.multiple_of(c * 512, 512), 512)],
                qx.at[rows(c * BLOCK), :], loc.at[2],
            ),
        )

    own_kv, own_d, own_q = own_copies()
    own_prompt = pltpu.make_async_copy(ptile, pt.at[g * N_CTX + c], loc.at[3])

    def start_kv(k, _):
        kv_copy(lax.rem(c + k, N_CTX)).start()
        return 0

    lax.fori_loop(1, N_CTX, start_kv, 0)
    own_kv.start()

    def prompt_copy(n):
        return remote(
            ptile, pt.at[g * N_CTX + c], p_s.at[n], p_r.at[g * N_CTX + c],
            (n // N_ULY, lax.rem(n, N_ULY), z),
        )

    def to_self(n):
        return is_diag & (n // N_ULY == g) & (lax.rem(n, N_ULY) == z)

    def from_self(n):
        return is_diag & (n // N_CTX == g) & (lax.rem(n, N_CTX) == c)

    def start_prompt(n, _):
        @pl.when(jnp.logical_not(to_self(n)))
        def _():
            prompt_copy(n).start()

        return 0

    lax.fori_loop(0, N_GRP * N_ULY, start_prompt, 0)

    @pl.when(is_diag)
    def _():
        own_prompt.start()

    def start_d(k, _):
        d_copy(lax.rem(c + k, N_CTX)).start()
        return 0

    lax.fori_loop(1, N_CTX, start_d, 0)
    own_d.start()

    def turn_heads(peer):
        for h in range(QH):
            at = pl.ds(pl.multiple_of(peer * 512 + h * 128, 128), 128)
            qrot[:, at] = turned(q_ref[:, at])

    def start_q(k, _):
        peer = lax.rem(c + k, N_CTX)
        turn_heads(peer)
        q_copy(peer).start()
        return 0

    lax.fori_loop(1, N_CTX, start_q, 0)
    turn_heads(c)
    own_q.start()

    def next_copy(j):
        return remote(
            kvw.at[rows(2 * CHUNK + j * BLOCK), :], kvw.at[rows(CHUNK + j * BLOCK), :],
            f_s.at[j], f_r.at[j], (g, jnp.where(has_next, z + 1, z - 1), c),
        )

    def far_copy(j):
        return remote(
            kvw.at[rows(CHUNK + j * BLOCK), :], kvw.at[rows(j * BLOCK), :],
            g_s.at[j], g_r.at[j], (g, jnp.where(has_next, z + 1, z - 1), c),
        )

    own_kv.wait()

    @pl.when(has_next)
    def _():
        next_copy(c).start()

    def pass_on(k, _):
        j = lax.rem(c + N_CTX - k, N_CTX)
        kv_arrival(j).wait_recv()

        @pl.when(has_next)
        def _():
            next_copy(j).start()

        return 0

    lax.fori_loop(1, N_CTX, pass_on, 0)

    def pass_far(k, _):
        j = lax.rem(c + N_CTX - k, N_CTX)

        @pl.when(has_prev)
        def _():
            next_copy(j).wait_recv()

        @pl.when(relays)
        def _():
            far_copy(j).start()

        return 0

    lax.fori_loop(0, N_CTX, pass_far, 0)

    def finish(k, _):
        j = lax.rem(c + k, N_CTX)
        kv_copy(j).wait_send()
        d_copy(j).wait_send()
        q_copy(j).wait_send()
        d_arrival(j).wait_recv()
        q_arrival(j).wait_recv()
        return 0

    lax.fori_loop(1, N_CTX, finish, 0)

    def finish_prompt(n, _):
        @pl.when(jnp.logical_not(to_self(n)))
        def _():
            prompt_copy(n).wait_send()

        @pl.when(jnp.logical_not(from_self(n)))
        def _():
            remote(ptile, pt.at[n], p_s.at[n], p_r.at[n], (n // N_ULY, lax.rem(n, N_ULY), z)).wait_recv()

        return 0

    lax.fori_loop(0, N_GRP * N_ULY, finish_prompt, 0)

    @pl.when(is_diag)
    def _():
        own_prompt.wait()

    own_d.wait()
    own_q.wait()

    def finish_far(j, _):
        @pl.when(has_next)
        def _():
            next_copy(j).wait_send()

        @pl.when(relays)
        def _():
            far_copy(j).wait_send()

        @pl.when(gets_far)
        def _():
            far_copy(j).wait_recv()

        return 0

    lax.fori_loop(0, N_CTX, finish_far, 0)


def dot_nt(a, b):
    return lax.dot_general(a, b, (((1,), (1,)), ((), ())), preferred_element_type=f32)


def dot_nn(a, b):
    return lax.dot_general(a, b, (((1,), (0,)), ((), ())), preferred_element_type=f32)


def dot_tn(a, b):
    return lax.dot_general(a, b, (((0,), (0,)), ((), ())), preferred_element_type=f32)


def attend(qx, dox, kvw, pt, len_ref, freq_t, ox, dqx, dkv, pg, s_all, kp, vp, pkg, pvg, o_t, dq_t):
    z = lax.axis_index("uly")
    zr = lax.rem(z, RUN_PLACES)
    run = z // RUN_PLACES
    start = zr * CHUNK
    for n in range(32):
        kp[4 * n : 4 * n + 4, :] = pt[n, 0:4, :]
        vp[4 * n : 4 * n + 4, :] = pt[n, 4:8, :]
    dkv[...] = jnp.zeros_like(dkv)
    pkg[...] = jnp.zeros_like(pkg)
    pvg[...] = jnp.zeros_like(pvg)

    def row_tile(r, _):
        t0 = r * TQ
        at_rows = pl.ds(pl.multiple_of(t0, TQ), TQ)
        q = jnp.concatenate([qx[at_rows, 128 * h : 128 * h + 128] for h in range(QH)], axis=0)
        do = jnp.concatenate([dox[at_rows, 128 * h : 128 * h + 128] for h in range(QH)], axis=0)
        tau = start + t0 + lax.broadcasted_iota(jnp.int32, (1, TQ), 1)
        begin = begins_of(tau, len_ref, run)
        pos = (PROMPT_TOKENS + tau - begin).astype(f32)
        to_win = 2 * CHUNK - start
        begin4 = jnp.concatenate([begin + to_win] * QH, axis=1)
        tau4 = jnp.concatenate([tau + to_win] * QH, axis=1)
        tile_hi = 2 * CHUNK // TK + r
        first = start + t0
        l0, l1, l2 = len_ref[run, 0], len_ref[run, 1], len_ref[run, 2]
        first_begin = (
            jnp.where(first >= l0, l0, 0)
            + jnp.where(first >= l0 + l1, l1, 0)
            + jnp.where(first >= l0 + l1 + l2, l2, 0)
        )
        tile_lo = (first_begin + to_win) // TK
        kpb, vpb = kp[...].astype(bf16), vp[...].astype(bf16)

        s = dot_nt(kpb, q)
        s_all[0:PROMPT_TOKENS, :] = s
        m0 = jnp.max(s, axis=0, keepdims=True)
        l_0 = jnp.sum(jnp.exp2((s - m0) * C2), axis=0, keepdims=True)

        def slot(kt):
            return pl.ds(pl.multiple_of(PROMPT_TOKENS + (kt - tile_lo) * TK, 128), TK)

        def keys(kt):
            return pl.ds(pl.multiple_of(kt * TK, TK), TK)

        def pass_a(kt, carry):
            m, l = carry
            s = dot_nt(kvw[keys(kt), 0:128], q)
            kidx = kt * TK + lax.broadcasted_iota(jnp.int32, (TK, LANES), 0)
            s = jnp.where((kidx >= begin4) & (kidx <= tau4), s, neg_fill)
            s_all[slot(kt), :] = s
            m_new = jnp.maximum(m, jnp.max(s, axis=0, keepdims=True))
            l = l * jnp.exp2((m - m_new) * C2) + jnp.sum(
                jnp.exp2((s - m_new) * C2), axis=0, keepdims=True
            )
            return m_new, l

        m, l = lax.fori_loop(tile_lo, tile_hi + 1, pass_a, (m0, l_0))
        inv_l = 1.0 / l

        def prob_of(s):
            return jnp.exp2((s - m) * C2) * inv_l

        p = prob_of(s_all[0:PROMPT_TOKENS, :])
        s_all[0:PROMPT_TOKENS, :] = p
        o_t[...] = dot_tn(vpb, p.astype(bf16))

        def pass_c(kt, _):
            p = prob_of(s_all[slot(kt), :])
            s_all[slot(kt), :] = p
            o_t[...] += dot_tn(kvw[keys(kt), 128:256], p.astype(bf16))
            return 0

        lax.fori_loop(tile_lo, tile_hi + 1, pass_c, 0)
        o = o_t[...].astype(bf16).astype(f32)
        delta = jnp.sum(o * do.astype(f32).T, axis=0, keepdims=True)
        o_rows = o.T.astype(bf16)
        for h in range(QH):
            ox[at_rows, 128 * h : 128 * h + 128] = o_rows[TQ * h : TQ * h + TQ, :]

        def grads(p, v):
            dp = dot_nt(v, do)
            return (p * (dp - delta) * SCALE).astype(bf16)

        p = s_all[0:PROMPT_TOKENS, :]
        ds = grads(p, vpb)
        dq_t[...] = dot_tn(kpb, ds)
        pkg[...] += dot_nn(ds, q)
        pvg[...] += dot_nn(p.astype(bf16), do)

        def pass_d(kt, _):
            p = s_all[slot(kt), :]
            ds = grads(p, kvw[keys(kt), 128:256])
            dq_t[...] += dot_tn(kvw[keys(kt), 0:128], ds)
            dkv[keys(kt), 0:128] += dot_nn(ds, q)
            dkv[keys(kt), 128:256] += dot_nn(p.astype(bf16), do)
            return 0

        lax.fori_loop(tile_lo, tile_hi + 1, pass_d, 0)
        angle = freq_t[...] * pos
        cosine = jnp.concatenate([jnp.cos(angle)] * QH, axis=1)
        sine = jnp.concatenate([jnp.sin(angle)] * QH, axis=1)
        x1, x2 = dq_t[0:64, :], dq_t[64:128, :]
        back = jnp.concatenate([x1 * cosine + x2 * sine, x2 * cosine - x1 * sine], axis=0)
        back = back.T.astype(bf16)
        for h in range(QH):
            dqx[at_rows, 128 * h : 128 * h + 128] = back[TQ * h : TQ * h + TQ, :]
        return 0

    lax.fori_loop(0, CHUNK // TQ, row_tile, 0)
    for n in range(32):
        pg[n, 0:4, :] = pkg[4 * n : 4 * n + 4, :]
        pg[n, 4:8, :] = pvg[4 * n : 4 * n + 4, :]


def send_out(
    ox, dqx, dkv, pg, len_ref, freq_ref,
    out, dq, dk, dv, dpk, dpv,
    far_out, far_in, near_out, near_in, own, pin, cosines, sines,
    o_s, o_r, q_s, q_r, f_s, f_r, n_s, n_r, k_s, k_r, v_s, v_r, p_s, p_r, loc,
):
    g, z, c = lax.axis_index("grp"), lax.axis_index("uly"), lax.axis_index("ctx")
    zr = lax.rem(z, RUN_PLACES)
    run = z // RUN_PLACES
    has_next, has_prev = zr < RUN_PLACES - 1, zr > 0
    gets_far = (zr == 1) | (zr == 2)
    sends_far = zr >= 2
    is_diag = z == c
    barrier = pltpu.get_barrier_semaphore()

    def greet(k, _):
        pl.semaphore_signal(barrier, inc=1, device_id=(g, z, lax.rem(c + k, N_CTX)), device_id_type=MESH)
        return 0

    lax.fori_loop(1, N_CTX, greet, 0)

    @pl.when(has_next)
    def _():
        pl.semaphore_signal(barrier, inc=1, device_id=(g, z + 1, c), device_id_type=MESH)

    def greet_prompt(n, _):
        gg, zz = n // N_ULY, lax.rem(n, N_ULY)

        @pl.when(jnp.logical_not(is_diag & (gg == g) & (zz == z)))
        def _():
            pl.semaphore_signal(barrier, inc=1, device_id=(gg, zz, z), device_id_type=MESH)

        return 0

    lax.fori_loop(0, N_GRP * N_ULY, greet_prompt, 0)

    def rows(at):
        return pl.ds(pl.multiple_of(at, BLOCK), BLOCK)

    far_out[...] = dkv[0:CHUNK, :].astype(bf16)

    targets = (
        (N_CTX - 1)
        + jnp.where(has_prev, 1, 0)
        + N_GRP * N_ULY
        - jnp.where(is_diag, 1, 0)
    )
    pl.semaphore_wait(barrier, targets)

    def remote(src, dst, s, r, dev):
        return pltpu.make_async_remote_copy(
            src_ref=src, dst_ref=dst, send_sem=s, recv_sem=r, device_id=dev, device_id_type=MESH
        )

    below = jnp.where(has_prev, z - 1, z + 1)

    def far_copy(j):
        return remote(
            far_out.at[rows(j * BLOCK), :], far_in.at[rows(j * BLOCK), :],
            f_s.at[j], f_r.at[j], (g, below, c),
        )

    def near_copy(j):
        return remote(
            near_out.at[rows(j * BLOCK), :], near_in.at[rows(j * BLOCK), :],
            n_s.at[j], n_r.at[j], (g, below, c),
        )

    def start_far(j, _):
        @pl.when(sends_far)
        def _():
            far_copy(j).start()

        return 0

    lax.fori_loop(0, N_CTX, start_far, 0)

    def block_copy(src, dst, s, r, width, peer):
        return remote(
            src.at[rows(peer * BLOCK), :],
            dst.at[:, pl.ds(pl.multiple_of(c * width, width), width)],
            s.at[peer], r.at[c], (g, z, peer),
        )

    def block_arrival(src, dst, s, r, width, j):
        return remote(
            src.at[rows(j * BLOCK), :],
            dst.at[:, pl.ds(pl.multiple_of(j * width, width), width)],
            s.at[j], r.at[j], (g, z, j),
        )

    def start_o(k, _):
        block_copy(ox, out, o_s, o_r, 512, lax.rem(c + k, N_CTX)).start()
        return 0

    def start_dq(k, _):
        block_copy(dqx, dq, q_s, q_r, 512, lax.rem(c + k, N_CTX)).start()
        return 0

    def own_copy(src, dst, width, at):
        return pltpu.make_async_copy(
            src.at[rows(c * BLOCK), :],
            dst.at[:, pl.ds(pl.multiple_of(c * width, width), width)], loc.at[at],
        )

    def to_self(n):
        return is_diag & (n // N_CTX == g) & (lax.rem(n, N_CTX) == c)

    def from_self(n):
        return is_diag & (n // N_ULY == g) & (lax.rem(n, N_ULY) == z)

    me = g * N_ULY + z

    def prompt_copy(n):
        return remote(
            pg.at[n], pin.at[me], p_s.at[n], p_r.at[me], (n // N_CTX, c, lax.rem(n, N_CTX))
        )

    def start_prompt(n, _):
        @pl.when(jnp.logical_not(to_self(n)))
        def _():
            prompt_copy(n).start()

        return 0

    lax.fori_loop(0, N_GRP * N_CTX, start_prompt, 0)
    own_prompt = pltpu.make_async_copy(pg.at[g * N_CTX + c], pin.at[me], loc.at[0])

    @pl.when(is_diag)
    def _():
        own_prompt.start()

    lax.fori_loop(1, N_CTX, start_o, 0)
    lax.fori_loop(1, N_CTX, start_dq, 0)
    own_copy(ox, out, 512, 1).start()
    own_copy(dqx, dq, 512, 2).start()

    def table(j, _):
        cosine, sine = cos_sin(zr * CHUNK + j * BLOCK, freq_ref, len_ref, run)
        cosines[rows(j * BLOCK), :] = cosine
        sines[rows(j * BLOCK), :] = sine
        return 0

    lax.fori_loop(0, N_CTX, table, 0)

    def near(j, _):
        mine = dkv[rows(CHUNK + j * BLOCK), :]

        @pl.when(gets_far)
        def _():
            far_copy(j).wait_recv()
            near_out[rows(j * BLOCK), :] = (mine + far_in[rows(j * BLOCK), :].astype(f32)).astype(bf16)

        @pl.when(jnp.logical_not(gets_far))
        def _():
            near_out[rows(j * BLOCK), :] = mine.astype(bf16)

        @pl.when(has_prev)
        def _():
            near_copy(j).start()

        return 0

    lax.fori_loop(0, N_CTX, near, 0)

    def finish_block(total, j):
        x = total[:, 0:128]
        cosine, sine = cosines[rows(j * BLOCK), :], sines[rows(j * BLOCK), :]
        own[0, rows(j * BLOCK), :] = (x * cosine - pltpu.roll(x, 64, 1) * sine).astype(bf16)
        own[1, rows(j * BLOCK), :] = total[:, 128:256].astype(bf16)

    def home(k, _):
        j = lax.rem(c + k, N_CTX)
        mine = dkv[rows(2 * CHUNK + j * BLOCK), :]

        @pl.when(has_next)
        def _():
            near_copy(j).wait_recv()
            finish_block(mine + near_in[rows(j * BLOCK), :].astype(f32), j)

        @pl.when(jnp.logical_not(has_next))
        def _():
            finish_block(mine, j)

        @pl.when(k < N_CTX)
        def _():
            block_copy(own.at[0], dk, k_s, k_r, 128, j).start()
            block_copy(own.at[1], dv, v_s, v_r, 128, j).start()

        return 0

    lax.fori_loop(1, N_CTX + 1, home, 0)
    own_copy(own.at[0], dk, 128, 3).start()
    own_copy(own.at[1], dv, 128, 4).start()

    def finish_prompt(n, _):
        @pl.when(jnp.logical_not(to_self(n)))
        def _():
            prompt_copy(n).wait_send()

        @pl.when(jnp.logical_not(from_self(n)))
        def _():
            remote(pg.at[n], pin.at[n], p_s.at[n], p_r.at[n], (n // N_CTX, c, lax.rem(n, N_CTX))).wait_recv()

        return 0

    lax.fori_loop(0, N_GRP * N_CTX, finish_prompt, 0)

    @pl.when(is_diag)
    def _():
        own_prompt.wait()

    total = jnp.sum(pin[...], axis=0)
    dpk[...] = total[0:4, :].astype(bf16)
    dpv[...] = total[4:8, :].astype(bf16)

    def finish(k, _):
        j = lax.rem(c + k, N_CTX)
        for src, dst, s, r, width in (
            (ox, out, o_s, o_r, 512),
            (dqx, dq, q_s, q_r, 512),
            (own.at[0], dk, k_s, k_r, 128),
            (own.at[1], dv, v_s, v_r, 128),
        ):
            block_copy(src, dst, s, r, width, j).wait_send()
            block_arrival(src, dst, s, r, width, j).wait_recv()
        return 0

    lax.fori_loop(1, N_CTX, finish, 0)
    own_copy(ox, out, 512, 1).wait()
    own_copy(dqx, dq, 512, 2).wait()
    own_copy(own.at[0], dk, 128, 3).wait()
    own_copy(own.at[1], dv, 128, 4).wait()

    def finish_z(j, _):
        @pl.when(sends_far)
        def _():
            far_copy(j).wait_send()

        @pl.when(has_prev)
        def _():
            near_copy(j).wait_send()

        return 0

    lax.fori_loop(0, N_CTX, finish_z, 0)


def spec(space):
    return pl.BlockSpec(memory_space=space)


VMEM, SMEM, ANY = pltpu.VMEM, pltpu.SMEM, pl.ANY
DMA = pltpu.SemaphoreType.DMA


def local(queries, keys_in, values_in, out_grad, lengths, prompt_keys, prompt_values):
    sds = jax.ShapeDtypeStruct
    lens = lengths[0]
    freq = frequencies()
    freq_row = jnp.asarray(np.tile(freq[None, :], (8, 1)))
    freq_col = jnp.asarray(np.tile(freq[:64, None], (1, TQ)))
    qx, dox, kvw, pt = pl.pallas_call(
        send_in,
        out_shape=(
            sds((CHUNK, 512), bf16),
            sds((CHUNK, 512), bf16),
            sds((WIN, 256), bf16),
            sds((32, 8, 128), f32),
        ),
        in_specs=[spec(VMEM), spec(ANY), spec(VMEM), spec(VMEM), spec(SMEM), spec(VMEM), spec(VMEM), spec(VMEM)],
        out_specs=(spec(ANY),) * 4,
        scratch_shapes=[
            VMEM((BLOCK, 4096), bf16),
            VMEM((BLOCK, 2048), bf16),
            VMEM((8, 128), f32),
        ]
        + [DMA((8,))] * 10
        + [DMA((32,))] * 2
        + [DMA((4,))],
        compiler_params=pltpu.CompilerParams(
            collective_id=0, has_side_effects=True, vmem_limit_bytes=32 << 20
        ),
        name="send_in",
    )(queries, out_grad, keys_in, values_in, lens, prompt_keys, prompt_values, freq_row)

    ox, dqx, dkv, pg = pl.pallas_call(
        attend,
        out_shape=(
            sds((CHUNK, 512), bf16),
            sds((CHUNK, 512), bf16),
            sds((WIN, 256), f32),
            sds((32, 8, 128), f32),
        ),
        in_specs=[spec(VMEM), spec(VMEM), spec(VMEM), spec(VMEM), spec(SMEM), spec(VMEM)],
        out_specs=(spec(VMEM),) * 4,
        scratch_shapes=[
            VMEM((PROMPT_TOKENS + 9 * TK, LANES), f32),
            VMEM((128, 128), f32),
            VMEM((128, 128), f32),
            VMEM((128, 128), f32),
            VMEM((128, 128), f32),
            VMEM((128, LANES), f32),
            VMEM((128, LANES), f32),
        ],
        compiler_params=pltpu.CompilerParams(vmem_limit_bytes=48 << 20),
        name="attend",
    )(qx, dox, kvw, pt, lens, freq_col)

    return pl.pallas_call(
        send_out,
        out_shape=(
            sds((BLOCK, 4096), bf16),
            sds((BLOCK, 4096), bf16),
            sds((BLOCK, 1024), bf16),
            sds((BLOCK, 1024), bf16),
            sds((4, 128), bf16),
            sds((4, 128), bf16),
        ),
        in_specs=[spec(ANY), spec(ANY), spec(VMEM), spec(ANY), spec(SMEM), spec(VMEM)],
        out_specs=(spec(ANY),) * 4 + (spec(VMEM),) * 2,
        scratch_shapes=[
            VMEM((CHUNK, 256), bf16),
            VMEM((CHUNK, 256), bf16),
            VMEM((CHUNK, 256), bf16),
            VMEM((CHUNK, 256), bf16),
            VMEM((2, CHUNK, 128), bf16),
            VMEM((32, 8, 128), f32),
            VMEM((CHUNK, 128), f32),
            VMEM((CHUNK, 128), f32),
        ]
        + [DMA((8,))] * 12
        + [DMA((32,))] * 2
        + [DMA((8,))],
        compiler_params=pltpu.CompilerParams(
            collective_id=1, has_side_effects=True, vmem_limit_bytes=32 << 20
        ),
        name="send_out",
    )(ox, dqx, dkv, pg, lens, freq_row)


def solution(mesh):
    tokens = P(("grp", "uly", "ctx"), None)
    prompt = P(("grp", "ctx"), "uly")
    in_specs = (tokens, tokens, tokens, tokens, P("grp", None, None), prompt, prompt)
    out_specs = (tokens, tokens, tokens, tokens, prompt, prompt)
    return jax.shard_map(local, mesh=mesh, in_specs=in_specs, out_specs=out_specs, check_vma=False)
```

time: 871 us -> 164 us (0.19)
  the two profiles are of different devices: /device:TPU:64 before, /device:TPU:216 now
where the time goes in v1:
time: 164 us; the launch traced here: 163 us
  Pallas kernels  148 us (90%)
  local copies, waits for them, and re-layouts  14.9 us (9%)
    pallas_call x1, Pallas kernels, local(): pl.pallas_call(send_out, out_shape=(sds((BLOCK, 4096), bf16), sds((BLOCK,...  68.2 us
    pallas_call x1, Pallas kernels, local(): pl.pallas_call(send_in, out_shape=(sds((CHUNK, 512), bf16), sds((CHUNK, 5...  42.6 us
    pallas_call x1, Pallas kernels, local(): pl.pallas_call(attend, out_shape=(sds((CHUNK, 512), bf16), sds((CHUNK, 51...  36.9 us
    unnamed x30, local copies, waits for them, and re-layouts  14.9 us

profile of v1, /device:TPU:216, one launch (start us, length us, event | category | flops | bytes accessed | tf_op | source)
XLA Modules:
  0.0 163.4 jit_solution(17597973430397388819)
XLA Ops:
  0.6 0.0 copy-start.1
  0.6 1.2 copy-done.1
  1.9 0.0 copy-start.2
  1.9 1.2 copy-done.2
  3.1 0.9 copy-done.3
  4.0 0.9 copy-done.4
  5.0 0.7 copy-done.6
  5.7 0.7 copy-done.8
  6.4 0.7 copy-done.10
  7.0 0.7 copy-done.11
  7.7 42.6 %send_in.1 = (bf16[1024,512]{1,0:T(8,128)(2,1)S(1)}, bf16[1024,512]{1,0:T(8,128)(2,1)S(1)}, bf16[3072,256]{1,0:T(8,128)(2,1)S(1)}, f32[32,8,128]{2,1,0:T(8,128)S(1)}) custom-call(bf16[128,4096]{1,0:T(8,128)(2,1)S(1)} %copy-done.1, bf16[128,4096]{1,0:T(8,128)(2,1)S(1)} %copy-done.2, bf16[128,1024]{1,0:T(8,128)(2,1)S(1)} %copy-done.3, ...), custom_call_target="tpu_custom_call" | custom-call | tf_op jit(solution)/shard_map/send_in/pallas_call | solution.py:715
  50.4 0.0 copy-start.5
  50.4 0.8 copy-done.5
  51.2 0.7 copy-done.9
  51.9 36.9 %attend.1 = (bf16[1024,512]{1,0:T(8,128)(2,1)S(1)}, bf16[1024,512]{1,0:T(8,128)(2,1)S(1)}, f32[3072,256]{1,0:T(8,128)}, f32[32,8,128]{2,1,0:T(8,128)S(1)}) custom-call(bf16[1024,512]{1,0:T(8,128)(2,1)S(1)} %get-tuple-element.14.qx, bf16[1024,512]{1,0:T(8,128)(2,1)S(1)} %get-tuple-element.15.dox, bf16[3072,256]{1,0:T(8,128)(2,1)S(1)} %get-tuple-element.16.kvw, ...), custom_call_target="tpu_custom_call" | custom-call | tf_op jit(solution)/shard_map/attend/pallas_call | solution.py:739
  88.8 0.0 copy-done.7
  88.8 1.9 %copy-done = f32[3072,256]{1,0:T(8,128)S(1)} copy-done((f32[3072,256]{1,0:T(8,128)S(1)}, f32[3072,256]{1,0:T(8,128)}, u32[]{:S(2)}) %copy-start) | copy-done | bytes 3145752
  90.7 68.2 %send_out.1 = (bf16[128,4096]{1,0:T(8,128)(2,1)S(1)}, bf16[128,4096]{1,0:T(8,128)(2,1)S(1)}, bf16[128,1024]{1,0:T(8,128)(2,1)S(1)}, bf16[128,1024]{1,0:T(8,128)(...) custom-call(bf16[1024,512]{1,0:T(8,128)(2,1)S(1)} %get-tuple-element.18.ox, ...), custom_call_target="tpu_custom_call" | custom-call | tf_op jit(solution)/shard_map/send_out/pallas_call | solution.py:762
  158.9 1.0 copy.21
  159.9 1.0 copy.22
  160.9 0.7 copy.23
  161.6 0.7 copy.24
  162.3 0.6 copy.25
  162.8 0.6 copy.26
  (9 shorter events, 0.0 us)
Async XLA Ops:
  0.6 1.2 copy-start.1
  1.9 1.2 copy-start.2
  3.1 0.9 copy-start.3
  4.0 0.9 copy-start.4
  5.0 0.7 copy-start.6
  5.7 0.7 copy-start.8
  6.4 0.7 copy-start.10
  7.0 0.7 copy-start.11
  7.7 81.1 %copy-start.7 = (f32[8,128]{1,0:T(8,128)S(1)}, f32[8,128]{1,0:T(8,128)}, u32[]{:S(2)}) copy-start(f32[8,128]{1,0:T(8,128)} %constant.4.clone.freq_ref) | copy-start | bytes 12292
  50.4 0.8 copy-start.5
  51.2 0.7 copy-start.9
  88.8 1.9 %copy-start = (f32[3072,256]{1,0:T(8,128)S(1)}, f32[3072,256]{1,0:T(8,128)}, u32[]{:S(2)}) copy-start(f32[3072,256]{1,0:T(8,128)} %get-tuple-element.20.dkv) | copy-start | bytes 9437188

commit v2 on v0

v2 whole, which is shorter than its diff:
```python
import jax
import jax.numpy as jnp
from jax import lax
from jax.experimental import pallas as pl
from jax.experimental.pallas import tpu as pltpu
from jax.sharding import PartitionSpec as P

H = 32
KEY_VALUE_HEADS = 8
HEAD_WIDTH = 128
PROMPT_TOKENS = 128
theta_base = 1000000.0
neg_fill = -1e30

N_GRP, N_ULY, N_CTX = 4, 8, 8
N_ALL = N_GRP * N_CTX
BLOCK = 128
CHUNK = N_CTX * BLOCK
RUN_PLACES = 4
QH = H // KEY_VALUE_HEADS
WIN = 3 * CHUNK
OWN = 2 * CHUNK
TQ = 256
ROW_TILES = CHUNK // TQ
LANES = QH * TQ
STEP = 512
HEAD_KEYS = PROMPT_TOKENS + TQ
HEAD_AT = WIN - TQ
SCALE = HEAD_WIDTH**-0.5
LOG2E = 1.4426950408889634
C2 = SCALE * LOG2E
MESH = pl.DeviceIdType.MESH
f32, bf16, i32 = jnp.float32, jnp.bfloat16, jnp.int32


def frequency_of(index):
    out = jnp.ones(index.shape, f32)
    for bit in range(6):
        power = theta_base ** (-(2.0 * 2**bit) / HEAD_WIDTH)
        out = out * jnp.where((index // 2**bit) % 2 == 1, f32(power), f32(1.0))
    return out


def begins_of(tau, lens):
    l0, l1, l2 = lens
    zero = jnp.zeros_like(tau)
    return (
        jnp.where(tau >= l0, l0, zero)
        + jnp.where(tau >= l0 + l1, l1, zero)
        + jnp.where(tau >= l0 + l1 + l2, l2, zero)
    )


def cos_sin(base, lens):
    tau = base + lax.broadcasted_iota(i32, (BLOCK, HEAD_WIDTH), 0)
    pos = PROMPT_TOKENS + tau - begins_of(tau, lens)
    lane = lax.broadcasted_iota(i32, (BLOCK, HEAD_WIDTH), 1)
    freq = frequency_of(lax.broadcasted_iota(i32, (8, HEAD_WIDTH), 1) % 64)[0:1, :]
    angle = pos.astype(f32) * freq
    sine = jnp.sin(angle)
    return jnp.cos(angle), jnp.where(lane < 64, -sine, sine)


def membership(base, lens, count):
    l0, l1, l2 = lens
    tau = base + lax.broadcasted_iota(i32, (count, HEAD_WIDTH), 0)
    lane = lax.broadcasted_iota(i32, (count, HEAD_WIDTH), 1)
    low = jnp.where(lane == 0, 0, jnp.where(lane == 1, l0, l0 + l1))
    high = jnp.where(lane == 0, l0, jnp.where(lane == 1, l0 + l1, l0 + l1 + l2))
    return (tau >= low) & (tau < high), lane


def dot_nt(a, b):
    return lax.dot_general(a, b, (((1,), (1,)), ((), ())), preferred_element_type=f32)


def dot_nn(a, b):
    return lax.dot_general(a, b, (((1,), (0,)), ((), ())), preferred_element_type=f32)


def dot_tn(a, b):
    return lax.dot_general(a, b, (((0,), (0,)), ((), ())), preferred_element_type=f32)


def step_kernel(
    q_hbm, do_hbm, k_hbm, v_hbm, len_ref, pk_ref, pv_ref,
    out, dq, dk, dv, dpk, dpv,
    q_in, k_in, v_in, qrot, kvs, ptile, pt, qx, dox, kvw, aug, onehot, qst, dost, kp, vp,
    s_all, o_t, dq_all, stats, dkv, pkg, pvg, pg, pin, ox, dqx,
    far_out, far_in, near_out, near_in, own, cosines, sines,
    q_s, q_r, d_s, d_r, kv_s, kv_r, f_s, f_r, g_s, g_r, o_s, o_r, dq_s, dq_r,
    fo_s, fo_r, no_s, no_r, k_s, k_r, v_s, v_r, p_s, p_r, pg_s, pg_r, loc,
):
    g, z, c = lax.axis_index("grp"), lax.axis_index("uly"), lax.axis_index("ctx")
    zr = lax.rem(z, RUN_PLACES)
    run = z // RUN_PLACES
    start = zr * CHUNK
    has_next, has_prev = zr < RUN_PLACES - 1, zr > 0
    middle = (zr == 1) | (zr == 2)
    has_far = zr >= 2
    is_diag = z == c
    lens = (len_ref[run, 0], len_ref[run, 1], len_ref[run, 2])
    barrier = pltpu.get_barrier_semaphore()

    def loop(low, high, body):
        def run_body(i, _):
            body(i)
            return 0

        lax.fori_loop(low, high, run_body, 0)

    def rows(at):
        return pl.ds(pl.multiple_of(at, BLOCK), BLOCK)

    def columns(at, width):
        return pl.ds(pl.multiple_of(at * width, width), width)

    def remote(src, dst, s, r, dev):
        return pltpu.make_async_remote_copy(
            src_ref=src, dst_ref=dst, send_sem=s, recv_sem=r, device_id=dev, device_id_type=MESH
        )

    load_k = pltpu.make_async_copy(k_hbm, k_in, loc.at[0])
    load_v = pltpu.make_async_copy(v_hbm, v_in, loc.at[1])
    load_q = pltpu.make_async_copy(q_hbm, q_in, loc.at[2])
    load_k.start()
    load_v.start()
    load_q.start()

    def greet(dev):
        pl.semaphore_signal(barrier, inc=1, device_id=dev, device_id_type=MESH)

    loop(1, N_CTX, lambda k: greet((g, z, lax.rem(c + k, N_CTX))))

    @pl.when(has_prev)
    def _():
        greet((g, z - 1, c))

    @pl.when(has_next)
    def _():
        greet((g, z + 1, c))

    def at_row(n):
        return n // N_CTX, c, lax.rem(n, N_CTX)

    def at_column(n):
        return n // N_ULY, lax.rem(n, N_ULY), z

    def row_is_me(n):
        return is_diag & (n // N_CTX == g) & (lax.rem(n, N_CTX) == c)

    def column_is_me(n):
        return is_diag & (n // N_ULY == g) & (lax.rem(n, N_ULY) == z)

    def greet_families(n):
        @pl.when(jnp.logical_not(row_is_me(n)))
        def _():
            greet(at_row(n))

        @pl.when(jnp.logical_not(column_is_me(n)))
        def _():
            greet(at_column(n))

    loop(0, N_ALL, greet_families)

    cosine, sine = cos_sin(start + c * BLOCK, lens)

    def turned(block):
        x = block.astype(f32)
        return (x * cosine + pltpu.roll(x, 64, 1) * sine).astype(bf16)

    load_k.wait()
    load_v.wait()
    for j in range(KEY_VALUE_HEADS):
        kvs[:, 256 * j : 256 * j + 128] = turned(k_in[:, 128 * j : 128 * j + 128])
        kvs[:, 256 * j + 128 : 256 * j + 256] = v_in[:, 128 * j : 128 * j + 128]
    ptile[0:4, :] = pk_ref[...].astype(f32)
    ptile[4:8, :] = pv_ref[...].astype(f32)

    pl.semaphore_wait(
        barrier,
        (N_CTX - 1)
        + jnp.where(has_next, 1, 0)
        + jnp.where(has_prev, 1, 0)
        + 2 * (N_ALL - jnp.where(is_diag, 1, 0)),
    )

    def spread(src, width, dst, base, s, r, peer):
        return remote(
            src.at[:, columns(peer, width)], dst.at[rows(base + c * BLOCK), :],
            s.at[peer], r.at[c], (g, z, peer),
        )

    def spread_in(src, width, dst, base, s, r, j):
        return remote(
            src.at[:, columns(j, width)], dst.at[rows(base + j * BLOCK), :], s.at[j], r.at[j], (g, z, j)
        )

    def spread_own(src, width, dst, base, at):
        return pltpu.make_async_copy(
            src.at[:, columns(c, width)], dst.at[rows(base + c * BLOCK), :], loc.at[at]
        )

    kv_way = (kvs, 256, kvw, OWN)
    d_way = (do_hbm, 512, dox, 0)
    q_way = (qrot, 512, qx, 0)
    loop(1, N_CTX, lambda k: spread(*kv_way, kv_s, kv_r, lax.rem(c + k, N_CTX)).start())
    spread_own(*kv_way, 3).start()
    me_in, me_back = g * N_CTX + c, g * N_ULY + z

    def prompt_copy(n):
        return remote(ptile, pt.at[me_in], p_s.at[n], p_r.at[me_in], at_column(n))

    def start_prompt(n):
        @pl.when(jnp.logical_not(column_is_me(n)))
        def _():
            prompt_copy(n).start()

    loop(0, N_ALL, start_prompt)
    own_prompt = pltpu.make_async_copy(ptile, pt.at[me_in], loc.at[4])

    @pl.when(is_diag)
    def _():
        own_prompt.start()

    loop(1, N_CTX, lambda k: spread(*d_way, d_s, d_r, lax.rem(c + k, N_CTX)).start())
    spread_own(*d_way, 5).start()
    load_q.wait()

    def turn_heads(peer):
        for h in range(QH):
            at = columns(peer * QH + h, 128)
            qrot[:, at] = turned(q_in[:, at])

    def start_q(k):
        peer = lax.rem(c + k, N_CTX)
        turn_heads(peer)
        spread(*q_way, q_s, q_r, peer).start()

    loop(1, N_CTX, start_q)
    turn_heads(c)
    spread_own(*q_way, 6).start()

    above = jnp.where(has_next, z + 1, z - 1)
    below = jnp.where(has_prev, z - 1, z + 1)

    def next_copy(j):
        return remote(
            kvw.at[rows(OWN + j * BLOCK), :], kvw.at[rows(CHUNK + j * BLOCK), :],
            f_s.at[j], f_r.at[j], (g, above, c),
        )

    def relay_copy(j):
        return remote(
            kvw.at[rows(CHUNK + j * BLOCK), :], kvw.at[rows(j * BLOCK), :],
            g_s.at[j], g_r.at[j], (g, above, c),
        )

    spread_own(*kv_way, 3).wait()

    @pl.when(has_next)
    def _():
        next_copy(c).start()

    def pass_on(k):
        j = lax.rem(c + N_CTX - k, N_CTX)
        spread_in(*kv_way, kv_s, kv_r, j).wait_recv()

        @pl.when(has_next)
        def _():
            next_copy(j).start()

    loop(1, N_CTX, pass_on)

    def tables(j):
        cosine_j, sine_j = cos_sin(start + j * BLOCK, lens)
        cosines[rows(j * BLOCK), :] = cosine_j
        sines[rows(j * BLOCK), :] = sine_j

    loop(0, N_CTX, tables)

    def key_masks(j):
        inside, lane = membership(start + j * BLOCK - OWN, lens, BLOCK)
        aug[rows(j * BLOCK), :] = jnp.where(inside | (lane >= 3), 0.0, neg_fill).astype(bf16)

    loop(0, WIN // BLOCK, key_masks)

    def query_masks(r):
        inside, lane = membership(start + r * TQ, lens, TQ)
        hot = jnp.where(inside & (lane < 3), 1.0, 0.0).astype(bf16)
        for h in range(QH):
            onehot[pl.ds(pl.multiple_of(r * LANES + h * TQ, TQ), TQ), :] = hot

    loop(0, ROW_TILES, query_masks)
    def clear(j):
        dkv[rows(j * BLOCK), :] = jnp.zeros((BLOCK, 256), f32)

    loop(0, WIN // BLOCK, clear)

    def take_prompt(n):
        @pl.when(jnp.logical_not(row_is_me(n)))
        def _():
            remote(ptile, pt.at[n], p_s.at[n], p_r.at[n], at_row(n)).wait_recv()

    loop(0, N_ALL, take_prompt)

    @pl.when(is_diag)
    def _():
        own_prompt.wait()

    for n in range(N_ALL):
        kp[4 * n : 4 * n + 4, :] = pt[n, 0:4, :]
        vp[4 * n : 4 * n + 4, :] = pt[n, 4:8, :]

    def pass_far(k):
        j = lax.rem(k + 4, N_CTX)

        @pl.when(has_prev)
        def _():
            next_copy(j).wait_recv()

        @pl.when(middle)
        def _():
            relay_copy(j).start()

    loop(0, N_CTX, pass_far)
    spread_own(*d_way, 5).wait()
    spread_own(*q_way, 6).wait()

    def keys_at(at, count):
        return pl.ds(pl.multiple_of(at, 256), count)

    def tile_rows(r):
        return pl.ds(pl.multiple_of(r * LANES, LANES), LANES)

    def masked_queries(r):
        return jnp.concatenate([onehot[tile_rows(r), :], qst[tile_rows(r), :]], axis=1)

    def masked_keys(at, count):
        return jnp.concatenate([aug[keys_at(at, count), :], kvw[keys_at(at, count), 0:128]], axis=1)

    def head_keys(r):
        first = jnp.concatenate([jnp.zeros((PROMPT_TOKENS, 128), bf16), kp[...].astype(bf16)], axis=1)
        return jnp.concatenate([first, masked_keys(OWN + r * TQ, TQ)], axis=0)

    def head_values(r):
        return jnp.concatenate([vp[...].astype(bf16), kvw[keys_at(OWN + r * TQ, TQ), 128:256]], axis=0)

    def head_scores(r, qa):
        s = dot_nt(head_keys(r), qa)
        key = lax.broadcasted_iota(i32, (HEAD_KEYS, LANES), 0) - PROMPT_TOKENS
        token = lax.broadcasted_iota(i32, (HEAD_KEYS, LANES), 1) % TQ
        return jnp.where(key <= token, s, neg_fill)

    head_at = pl.ds(HEAD_AT, HEAD_KEYS)

    def first_step(r):
        return jnp.where(has_far, r // 2, jnp.where(has_prev, CHUNK // STEP, OWN // STEP))

    def forward(k):
        r = ROW_TILES - 1 - k

        @pl.when(has_far & (lax.rem(k, 2) == 0))
        def _():
            loop(0, 4, lambda j: relay_copy(4 - 2 * k + j).wait_recv())

        for e in range(2):
            j = 2 * r + e

            @pl.when(j != c)
            def _():
                spread_in(*d_way, d_s, d_r, j).wait_recv()
                spread_in(*q_way, q_s, q_r, j).wait_recv()

        at_rows = pl.ds(pl.multiple_of(r * TQ, TQ), TQ)
        for h in range(QH):
            to = pl.ds(pl.multiple_of(r * LANES + h * TQ, TQ), TQ)
            qst[to, :] = qx[at_rows, 128 * h : 128 * h + 128]
            dost[to, :] = dox[at_rows, 128 * h : 128 * h + 128]
        qa = masked_queries(r)
        low = first_step(r)

        s = head_scores(r, qa)
        s_all[head_at, :] = s
        top = jnp.max(s, axis=0, keepdims=True)

        def score(at, count, top):
            s = dot_nt(masked_keys(at, count), qa)
            s_all[keys_at(at, count), :] = s
            return jnp.maximum(top, jnp.max(s, axis=0, keepdims=True))

        top = lax.fori_loop(0, r, lambda t, a: score(OWN + t * TQ, TQ, a), top)
        top = lax.fori_loop(low, OWN // STEP, lambda t, a: score(t * STEP, STEP, a), top)
        top = top * C2

        def power(at, total):
            p = jnp.exp2(s_all[at, :] * C2 - top)
            s_all[at, :] = p
            return total + jnp.sum(p, axis=0, keepdims=True)

        total = power(head_at, jnp.zeros((1, LANES), f32))
        total = lax.fori_loop(0, r, lambda t, a: power(keys_at(OWN + t * TQ, TQ), a), total)
        total = lax.fori_loop(low, OWN // STEP, lambda t, a: power(keys_at(t * STEP, STEP), a), total)
        inverse = 1.0 / total
        o_t[...] = dot_tn(head_values(r), (s_all[head_at, :] * inverse).astype(bf16))

        def gather(at, count):
            half = (s_all[keys_at(at, count), :] * inverse).astype(bf16)
            o_t[...] += dot_tn(kvw[keys_at(at, count), 128:256], half)

        loop(0, r, lambda t: gather(OWN + t * TQ, TQ))
        loop(low, OWN // STEP, lambda t: gather(t * STEP, STEP))
        o = o_t[...].astype(bf16).astype(f32)
        delta = jnp.sum(o * dost[tile_rows(r), :].astype(f32).T, axis=0, keepdims=True)
        stats[r, 0:1, :] = top + jnp.log(total) * LOG2E
        stats[r, 1:2, :] = delta
        o_rows = o.T.astype(bf16)
        for h in range(QH):
            ox[at_rows, 128 * h : 128 * h + 128] = o_rows[TQ * h : TQ * h + TQ, :]
        dq_all[r] = jnp.zeros((128, LANES), f32)
        send_rows(ox, out, o_s, o_r, r, 7)

    def home(src, dst, s, r, width, peer):
        return remote(
            src.at[rows(peer * BLOCK), :], dst.at[:, columns(c, width)], s.at[peer], r.at[c], (g, z, peer)
        )

    def home_in(src, dst, s, r, width, j):
        return remote(
            src.at[rows(j * BLOCK), :], dst.at[:, columns(j, width)], s.at[j], r.at[j], (g, z, j)
        )

    def home_own(src, dst, width, at):
        return pltpu.make_async_copy(src.at[rows(c * BLOCK), :], dst.at[:, columns(c, width)], loc.at[at])

    def send_rows(src, dst, s, rs, r, at):
        for e in range(2):
            j = 2 * r + e

            @pl.when(j != c)
            def _():
                home(src, dst, s, rs, 512, j).start()

            @pl.when(j == c)
            def _():
                home_own(src, dst, 512, at).start()

    loop(0, ROW_TILES, forward)

    def grads(r, s, v):
        p = jnp.exp2(s * C2 - stats[r, 0:1, :])
        dp = dot_nt(v, dost[tile_rows(r), :])
        ds = (p * (dp - stats[r, 1:2, :]) * SCALE).astype(bf16)
        return p.astype(bf16), ds

    def backward(r, at, count):
        s = dot_nt(masked_keys(at, count), masked_queries(r))
        here = keys_at(at, count)
        half, ds = grads(r, s, kvw[here, 128:256])
        dq_all[r] += dot_tn(kvw[here, 0:128], ds)
        dkv[here, 0:128] += dot_nn(ds, qst[tile_rows(r), :])
        dkv[here, 128:256] += dot_nn(half, dost[tile_rows(r), :])

    @pl.when(has_far)
    def _():
        def far_rows(r):
            loop(r // 2, CHUNK // STEP, lambda t: backward(r, t * STEP, STEP))

        loop(0, ROW_TILES, far_rows)

    def far_copy(j):
        return remote(
            far_out.at[rows(j * BLOCK), :], far_in.at[rows(j * BLOCK), :], fo_s.at[j], fo_r.at[j], (g, below, c)
        )

    def near_copy(j):
        return remote(
            near_out.at[rows(j * BLOCK), :], near_in.at[rows(j * BLOCK), :], no_s.at[j], no_r.at[j], (g, below, c)
        )

    def send_far(j):
        @pl.when(has_far)
        def _():
            far_out[rows(j * BLOCK), :] = dkv[rows(j * BLOCK), :].astype(bf16)
            far_copy(j).start()

    loop(0, N_CTX, send_far)

    @pl.when(has_prev)
    def _():
        def near_rows(r):
            loop(CHUNK // STEP, OWN // STEP, lambda t: backward(r, t * STEP, STEP))

        loop(0, ROW_TILES, near_rows)

    def send_near(j):
        mine = dkv[rows(CHUNK + j * BLOCK), :]

        @pl.when(middle)
        def _():
            far_copy(j).wait_recv()
            near_out[rows(j * BLOCK), :] = (mine + far_in[rows(j * BLOCK), :].astype(f32)).astype(bf16)

        @pl.when(jnp.logical_not(middle))
        def _():
            near_out[rows(j * BLOCK), :] = mine.astype(bf16)

        @pl.when(has_prev)
        def _():
            near_copy(j).start()

    loop(0, N_CTX, send_near)

    pkg[...] = jnp.zeros((128, 128), f32)
    pvg[...] = jnp.zeros((128, 128), f32)

    def own_rows(k):
        r = lax.rem(c // 2 + k, ROW_TILES)
        loop(0, r, lambda t: backward(r, OWN + t * TQ, TQ))
        s = head_scores(r, masked_queries(r))
        half, ds = grads(r, s, head_values(r))
        k_head = jnp.concatenate([kp[...].astype(bf16), kvw[keys_at(OWN + r * TQ, TQ), 0:128]], axis=0)
        back = dq_all[r] + dot_tn(k_head, ds)
        k_part = dot_nn(ds, qst[tile_rows(r), :])
        v_part = dot_nn(half, dost[tile_rows(r), :])
        pkg[...] += k_part[0:PROMPT_TOKENS, :]
        pvg[...] += v_part[0:PROMPT_TOKENS, :]
        here = keys_at(OWN + r * TQ, TQ)
        dkv[here, 0:128] += k_part[PROMPT_TOKENS:HEAD_KEYS, :]
        dkv[here, 128:256] += v_part[PROMPT_TOKENS:HEAD_KEYS, :]
        tau = start + r * TQ + lax.broadcasted_iota(i32, (1, TQ), 1)
        pos = (PROMPT_TOKENS + tau - begins_of(tau, lens)).astype(f32)
        angle = frequency_of(lax.broadcasted_iota(i32, (64, TQ), 0)) * pos
        cosine_t = jnp.concatenate([jnp.cos(angle)] * QH, axis=1)
        sine_t = jnp.concatenate([jnp.sin(angle)] * QH, axis=1)
        x1, x2 = back[0:64, :], back[64:128, :]
        turned_back = jnp.concatenate([x1 * cosine_t + x2 * sine_t, x2 * cosine_t - x1 * sine_t], axis=0)
        q_rows = turned_back.T.astype(bf16)
        at_rows = pl.ds(pl.multiple_of(r * TQ, TQ), TQ)
        for h in range(QH):
            dqx[at_rows, 128 * h : 128 * h + 128] = q_rows[TQ * h : TQ * h + TQ, :]
        send_rows(dqx, dq, dq_s, dq_r, r, 8)

    loop(0, ROW_TILES, own_rows)

    for n in range(N_ALL):
        pg[n, 0:4, :] = pkg[4 * n : 4 * n + 4, :]
        pg[n, 4:8, :] = pvg[4 * n : 4 * n + 4, :]

    def prompt_back(n):
        return remote(pg.at[n], pin.at[me_back], pg_s.at[n], pg_r.at[me_back], at_row(n))

    def start_back(n):
        @pl.when(jnp.logical_not(row_is_me(n)))
        def _():
            prompt_back(n).start()

    loop(0, N_ALL, start_back)
    own_back = pltpu.make_async_copy(pg.at[me_in], pin.at[me_back], loc.at[9])

    @pl.when(is_diag)
    def _():
        own_back.start()

    def finish_block(total, j):
        x = total[:, 0:128]
        cosine_j, sine_j = cosines[rows(j * BLOCK), :], sines[rows(j * BLOCK), :]
        own[0, rows(j * BLOCK), :] = (x * cosine_j - pltpu.roll(x, 64, 1) * sine_j).astype(bf16)
        own[1, rows(j * BLOCK), :] = total[:, 128:256].astype(bf16)

    def send_own(k):
        j = lax.rem(c + k, N_CTX)
        mine = dkv[rows(OWN + j * BLOCK), :]

        @pl.when(has_next)
        def _():
            near_copy(j).wait_recv()
            finish_block(mine + near_in[rows(j * BLOCK), :].astype(f32), j)

        @pl.when(jnp.logical_not(has_next))
        def _():
            finish_block(mine, j)

        @pl.when(k < N_CTX)
        def _():
            home(own.at[0], dk, k_s, k_r, 128, j).start()
            home(own.at[1], dv, v_s, v_r, 128, j).start()

    loop(1, N_CTX + 1, send_own)
    home_own(own.at[0], dk, 128, 10).start()
    home_own(own.at[1], dv, 128, 11).start()

    def finish_prompt(n):
        @pl.when(jnp.logical_not(column_is_me(n)))
        def _():
            prompt_copy(n).wait_send()
            remote(pg.at[n], pin.at[n], pg_s.at[n], pg_r.at[n], at_column(n)).wait_recv()

        @pl.when(jnp.logical_not(row_is_me(n)))
        def _():
            prompt_back(n).wait_send()

    loop(0, N_ALL, finish_prompt)

    @pl.when(is_diag)
    def _():
        own_back.wait()

    total = jnp.sum(pin[...], axis=0)
    dpk[...] = total[0:4, :].astype(bf16)
    dpv[...] = total[4:8, :].astype(bf16)

    backs = (
        (ox, out, o_s, o_r, 512),
        (dqx, dq, dq_s, dq_r, 512),
        (own.at[0], dk, k_s, k_r, 128),
        (own.at[1], dv, v_s, v_r, 128),
    )

    def finish(k):
        j = lax.rem(c + k, N_CTX)
        spread(*kv_way, kv_s, kv_r, j).wait_send()
        spread(*d_way, d_s, d_r, j).wait_send()
        spread(*q_way, q_s, q_r, j).wait_send()
        for back in backs:
            home(*back, j).wait_send()
            home_in(*back, j).wait_recv()

    loop(1, N_CTX, finish)
    for at, (src, dst, _, _, width) in zip((7, 8, 10, 11), backs):
        home_own(src, dst, width, at).wait()

    def finish_z(j):
        @pl.when(has_next)
        def _():
            next_copy(j).wait_send()

        @pl.when(middle)
        def _():
            relay_copy(j).wait_send()

        @pl.when(has_far)
        def _():
            far_copy(j).wait_send()

        @pl.when(has_prev)
        def _():
            near_copy(j).wait_send()

    loop(0, N_CTX, finish_z)


def place(*refs):
    sems = refs[-1]
    count = (len(refs) - 1) // 2
    copies = [pltpu.make_async_copy(refs[i], refs[count + i], sems.at[i]) for i in range(count)]
    for copy in copies:
        copy.start()
    for copy in copies:
        copy.wait()


def spec(space):
    return pl.BlockSpec(memory_space=space)


VMEM, SMEM, HBM, ANY = pltpu.VMEM, pltpu.SMEM, pltpu.HBM, pl.ANY
DMA = pltpu.SemaphoreType.DMA


def local(queries, keys_in, values_in, out_grad, lengths, prompt_keys, prompt_values):
    sds = jax.ShapeDtypeStruct
    shapes = (
        sds((BLOCK, 4096), bf16),
        sds((BLOCK, 4096), bf16),
        sds((BLOCK, 1024), bf16),
        sds((BLOCK, 1024), bf16),
        sds((4, 128), bf16),
        sds((4, 128), bf16),
    )
    results = pl.pallas_call(
        step_kernel,
        out_shape=shapes,
        in_specs=[spec(HBM)] * 4 + [spec(SMEM), spec(VMEM), spec(VMEM)],
        out_specs=(spec(VMEM),) * 6,
        scratch_shapes=[
            VMEM((BLOCK, 4096), bf16),
            VMEM((BLOCK, 1024), bf16),
            VMEM((BLOCK, 1024), bf16),
            VMEM((BLOCK, 4096), bf16),
            VMEM((BLOCK, 2048), bf16),
            VMEM((8, 128), f32),
            VMEM((N_ALL, 8, 128), f32),
            VMEM((CHUNK, 512), bf16),
            VMEM((CHUNK, 512), bf16),
            VMEM((WIN, 256), bf16),
            VMEM((WIN, 128), bf16),
            VMEM((ROW_TILES * LANES, 128), bf16),
            VMEM((ROW_TILES * LANES, 128), bf16),
            VMEM((ROW_TILES * LANES, 128), bf16),
            VMEM((128, 128), f32),
            VMEM((128, 128), f32),
            VMEM((HEAD_AT + HEAD_KEYS, LANES), f32),
            VMEM((128, LANES), f32),
            VMEM((ROW_TILES, 128, LANES), f32),
            VMEM((ROW_TILES, 8, LANES), f32),
            VMEM((WIN, 256), f32),
            VMEM((128, 128), f32),
            VMEM((128, 128), f32),
            VMEM((N_ALL, 8, 128), f32),
            VMEM((N_ALL, 8, 128), f32),
            VMEM((CHUNK, 512), bf16),
            VMEM((CHUNK, 512), bf16),
        ]
        + [VMEM((CHUNK, 256), bf16)] * 4
        + [VMEM((2, CHUNK, 128), bf16), VMEM((CHUNK, 128), f32), VMEM((CHUNK, 128), f32)]
        + [DMA((8,))] * 22
        + [DMA((N_ALL,))] * 4
        + [DMA((12,))],
        compiler_params=pltpu.CompilerParams(
            collective_id=0, has_side_effects=True, vmem_limit_bytes=56 << 20
        ),
        name="grpo_step",
    )(queries, out_grad, keys_in, values_in, lengths[0], prompt_keys, prompt_values)
    return pl.pallas_call(
        place,
        out_shape=shapes,
        in_specs=[spec(VMEM)] * 6,
        out_specs=(spec(HBM),) * 6,
        scratch_shapes=[DMA((6,))],
        name="place",
    )(*results)


def solution(mesh):
    tokens = P(("grp", "uly", "ctx"), None)
    prompt = P(("grp", "ctx"), "uly")
    in_specs = (tokens, tokens, tokens, tokens, P("grp", None, None), prompt, prompt)
    out_specs = (tokens, tokens, tokens, tokens, prompt, prompt)
    return jax.shard_map(local, mesh=mesh, in_specs=in_specs, out_specs=out_specs, check_vma=False)
```

time: 871 us -> 128 us (0.15)
  local copies, waits for them, and re-layouts: 245 us -> 0 us
  waiting for transfers between devices: 243 us -> 0 us
  blocking collectives: 128 us -> 0 us
  Pallas kernels: 0 us -> 126 us
  matrix products: 90.9 us -> 0 us
  other arithmetic: 84.3 us -> 0 us
  starting transfers between devices: 51.4 us -> 0 us
  between operations: 14.8 us -> 0.64 us
    all_to_all x8 -> x0, waiting for transfers between devices: 190 us -> none  [the longest x1 39.7 us: local(): lax.all_to_all(key_running_sum.reshape(group_tokens, -1).astype(jnp.bfloa...]
    all_gather x2 -> x0, blocking collectives: 128 us -> none  [the longest x1 66.5 us: local(): lax.all_gather(prompt_keys, ('grp', 'ctx'), axis=0, tiled=True)]
    pallas_call x0 -> x2, Pallas kernels: none -> 126 us  [the longest x1 122 us: local(): pl.pallas_call(step_kernel, out_shape=shapes, in_specs=[spec(HBM)] * 4 +...]
    dynamic_update_slice x48 -> x0, local copies, waits for them, and re-layouts: 118 us -> none  [the longest x16 56.6 us: step_block(): lax.dynamic_update_slice_in_dim(key_running_sum, lax.dynamic_slice_in_dim...]
    dot_general x48 -> x0, matrix products: 90.9 us -> none  [the longest x8 22.9 us: attend_block(): jnp.einsum('hgqk,qhgd->khd', prob_half, grad_blk, preferred_element_type=...]
    dynamic_slice x48 -> x0, local copies, waits for them, and re-layouts: 64.7 us -> none  [the longest x16 40 us: step_block(): lax.dynamic_slice_in_dim(key_running_sum, window_start, window, 0)]
    add x41 -> x0, other arithmetic: 52.9 us -> none  [the longest x8 21.1 us: step_block(): lax.dynamic_slice_in_dim(value_running_sum, window_start, window, 0)]
    all_to_all x8 -> x0, starting transfers between devices: 51.3 us -> none  [the longest x1 8.25 us: local(): lax.all_to_all(queries, 'uly', split_axis=1, concat_axis=0, tiled=True)]
  transfers between devices with their start and end apart: 13 -> 0, of which waited for: 9 -> 0; matrix products, arithmetic and copies ran while one was open for 7% -> 0% of each run, Pallas kernels for 0% -> 0%
where the time goes in v2:
time: 128 us; the launch traced here: 126 us
  Pallas kernels  126 us (98%)
    pallas_call x1, Pallas kernels, local(): pl.pallas_call(step_kernel, out_shape=shapes, in_specs=[spec(HBM)] * 4 +...  122 us
    pallas_call x1, Pallas kernels, local(): pl.pallas_call(place, out_shape=shapes, in_specs=[spec(VMEM)] * 6, out_sp...  3.2 us

profile of v2, /device:TPU:64, one launch (start us, length us, event | category | flops | bytes accessed | tf_op | source)
XLA Modules:
  0.0 126.2 jit_solution(13223181060399608006)
XLA Ops:
  0.6 122.4 %grpo_step.1 = (bf16[128,4096]{1,0:T(8,128)(2,1)}, bf16[128,4096]{1,0:T(8,128)(2,1)}, bf16[128,1024]{1,0:T(8,128)(2,1)}, bf16[128,1024]{1,0:T(8,128)(2,1)}, bf16...) custom-call(bf16[128,4096]{1,0:T(8,128)(2,1)} %q_hbm.1, bf16[128,4096]{1,0:T(8,128)(2,1)} %do_hbm.1, bf16[128,1024]{1,0:T(8,128)(2,1)} %k_hbm.1, ...), custom_call_target="tpu_custom_call" | custom-call | tf_op jit(solution)/shard_map/grpo_step/pallas_call | solution.py:681
  123.0 3.2 %place.1 = (bf16[128,4096]{1,0:T(8,128)(2,1)}, bf16[128,4096]{1,0:T(8,128)(2,1)}, bf16[128,1024]{1,0:T(8,128)(2,1)}, bf16[128,1024]{1,0:T(8,128)(2,1)}, bf16[4,128]{1,0:T(4,128)(2,1)}, /*index=5*/bf16[4,128]{1,0:T(4,128)(2,1)}) custom-call(bf16[128,4096]{1,0:T(8,128)(2,1)} %get-tuple-element.12.refs_0_, bf16[128,4096]{1,0:T(8,128)(2,1)} %get-tuple-element.13.refs_1_, ...), custom_call_target="tpu_custom_call" | custom-call | tf_op jit(solution)/shard_map/place/pallas_call | solution.py:725

commit v3 on v2

--- a/solution.py
+++ b/solution.py
@@ -13,7 +13,6 @@
 neg_fill = -1e30
 
 N_GRP, N_ULY, N_CTX = 4, 8, 8
-N_ALL = N_GRP * N_CTX
 BLOCK = 128
 CHUNK = N_CTX * BLOCK
 RUN_PLACES = 4
@@ -83,13 +82,13 @@
 
 
 def step_kernel(
-    q_hbm, do_hbm, k_hbm, v_hbm, len_ref, pk_ref, pv_ref,
+    q_hbm, do_hbm, k_hbm, v_hbm, len_ref, pk_hbm, pv_hbm,
     out, dq, dk, dv, dpk, dpv,
-    q_in, k_in, v_in, qrot, kvs, ptile, pt, qx, dox, kvw, aug, onehot, qst, dost, kp, vp,
-    s_all, o_t, dq_all, stats, dkv, pkg, pvg, pg, pin, ox, dqx,
+    q_in, k_in, v_in, pk_in, pv_in, qrot, kvs, ptile, pta, rows64, pb, qx, dox, kvw, aug, onehot, qst, dost, kp, vp,
+    s_all, o_t, dq_all, stats, dkv, pkg, pvg, pgb, pgin, tot, bin, ft, pfin, ox, dqx,
     far_out, far_in, near_out, near_in, own, cosines, sines,
     q_s, q_r, d_s, d_r, kv_s, kv_r, f_s, f_r, g_s, g_r, o_s, o_r, dq_s, dq_r,
-    fo_s, fo_r, no_s, no_r, k_s, k_r, v_s, v_r, p_s, p_r, pg_s, pg_r, loc,
+    fo_s, fo_r, no_s, no_r, k_s, k_r, v_s, v_r, p_s, p_r, pb_s, pb_r, pc_s, pc_r, ga_s, ga_r, gb_s, gb_r, gc_s, gc_r, loc,
 ):
     g, z, c = lax.axis_index("grp"), lax.axis_index("uly"), lax.axis_index("ctx")
     zr = lax.rem(z, RUN_PLACES)
@@ -126,6 +125,10 @@
     load_k.start()
     load_v.start()
     load_q.start()
+    load_pk = pltpu.make_async_copy(pk_hbm, pk_in, loc.at[12])
+    load_pv = pltpu.make_async_copy(pv_hbm, pv_in, loc.at[13])
+    load_pk.start()
+    load_pv.start()
 
     def greet(dev):
         pl.semaphore_signal(barrier, inc=1, device_id=dev, device_id_type=MESH)
@@ -140,28 +143,16 @@
     def _():
         greet((g, z + 1, c))
 
-    def at_row(n):
-        return n // N_CTX, c, lax.rem(n, N_CTX)
-
-    def at_column(n):
-        return n // N_ULY, lax.rem(n, N_ULY), z
-
-    def row_is_me(n):
-        return is_diag & (n // N_CTX == g) & (lax.rem(n, N_CTX) == c)
-
-    def column_is_me(n):
-        return is_diag & (n // N_ULY == g) & (lax.rem(n, N_ULY) == z)
-
-    def greet_families(n):
-        @pl.when(jnp.logical_not(row_is_me(n)))
-        def _():
-            greet(at_row(n))
-
-        @pl.when(jnp.logical_not(column_is_me(n)))
-        def _():
-            greet(at_column(n))
-
-    loop(0, N_ALL, greet_families)
+    hub = (g, c, c)
+
+    @pl.when(is_diag)
+    def _():
+        loop(1, N_ULY, lambda k: greet((g, lax.rem(z + k, N_ULY), c)))
+        loop(1, N_GRP, lambda k: greet((lax.rem(g + k, N_GRP), z, c)))
+
+    @pl.when(jnp.logical_not(is_diag))
+    def _():
+        greet(hub)
 
     cosine, sine = cos_sin(start + c * BLOCK, lens)
 
@@ -174,15 +165,17 @@
     for j in range(KEY_VALUE_HEADS):
         kvs[:, 256 * j : 256 * j + 128] = turned(k_in[:, 128 * j : 128 * j + 128])
         kvs[:, 256 * j + 128 : 256 * j + 256] = v_in[:, 128 * j : 128 * j + 128]
-    ptile[0:4, :] = pk_ref[...].astype(f32)
-    ptile[4:8, :] = pv_ref[...].astype(f32)
+    load_pk.wait()
+    load_pv.wait()
+    ptile[0:4, :] = pk_in[...].astype(f32)
+    ptile[4:8, :] = pv_in[...].astype(f32)
 
     pl.semaphore_wait(
         barrier,
         (N_CTX - 1)
         + jnp.where(has_next, 1, 0)
         + jnp.where(has_prev, 1, 0)
-        + 2 * (N_ALL - jnp.where(is_diag, 1, 0)),
+        + jnp.where(is_diag, N_ULY - 1 + N_GRP - 1, 1),
     )
 
     def spread(src, width, dst, base, s, r, peer):
@@ -206,25 +199,24 @@
     q_way = (qrot, 512, qx, 0)
     loop(1, N_CTX, lambda k: spread(*kv_way, kv_s, kv_r, lax.rem(c + k, N_CTX)).start())
     spread_own(*kv_way, 3).start()
-    me_in, me_back = g * N_CTX + c, g * N_ULY + z
-
-    def prompt_copy(n):
-        return remote(ptile, pt.at[me_in], p_s.at[n], p_r.at[me_in], at_column(n))
-
-    def start_prompt(n):
-        @pl.when(jnp.logical_not(column_is_me(n)))
-        def _():
-            prompt_copy(n).start()
-
-    loop(0, N_ALL, start_prompt)
-    own_prompt = pltpu.make_async_copy(ptile, pt.at[me_in], loc.at[4])
-
-    @pl.when(is_diag)
-    def _():
-        own_prompt.start()
-
-    loop(1, N_CTX, lambda k: spread(*d_way, d_s, d_r, lax.rem(c + k, N_CTX)).start())
-    spread_own(*d_way, 5).start()
+
+    def tile_copy(at):
+        return remote(ptile, pta.at[at], p_s.at[0], p_r.at[at], (g, z, z))
+
+    def group_copy(at, k):
+        return remote(pb.at[at], pb.at[at], pb_s.at[k], pb_r.at[at], (lax.rem(g + k, N_GRP), z, c))
+
+    def column_copy(k):
+        return remote(pb, pb, pc_s.at[k], pc_r.at[0], (g, lax.rem(z + k, N_ULY), c))
+
+    @pl.when(is_diag)
+    def _():
+        pta[c] = ptile[...]
+
+    @pl.when(jnp.logical_not(is_diag))
+    def _():
+        tile_copy(c).start()
+
     load_q.wait()
 
     def turn_heads(peer):
@@ -241,6 +233,15 @@
     turn_heads(c)
     spread_own(*q_way, 6).start()
 
+    @pl.when(is_diag)
+    def _():
+        loop(1, N_CTX, lambda k: tile_copy(lax.rem(c + k, N_CTX)).wait_recv())
+        for n in range(N_CTX):
+            rows64[4 * n : 4 * n + 4, :] = pta[n, 0:4, :]
+            rows64[32 + 4 * n : 36 + 4 * n, :] = pta[n, 4:8, :]
+        pb[g] = rows64[...].astype(bf16)
+        loop(1, N_GRP, lambda k: group_copy(g, k).start())
+
     above = jnp.where(has_next, z + 1, z - 1)
     below = jnp.where(has_prev, z - 1, z + 1)
 
@@ -271,6 +272,13 @@
             next_copy(j).start()
 
     loop(1, N_CTX, pass_on)
+    loop(1, N_CTX, lambda k: spread(*d_way, d_s, d_r, lax.rem(c + k, N_CTX)).start())
+    spread_own(*d_way, 5).start()
+
+    @pl.when(is_diag)
+    def _():
+        loop(1, N_GRP, lambda k: group_copy(lax.rem(g + k, N_GRP), k).wait_recv())
+        loop(1, N_ULY, lambda k: column_copy(k).start())
 
     def tables(j):
         cosine_j, sine_j = cos_sin(start + j * BLOCK, lens)
@@ -297,21 +305,6 @@
 
     loop(0, WIN // BLOCK, clear)
 
-    def take_prompt(n):
-        @pl.when(jnp.logical_not(row_is_me(n)))
-        def _():
-            remote(ptile, pt.at[n], p_s.at[n], p_r.at[n], at_row(n)).wait_recv()
-
-    loop(0, N_ALL, take_prompt)
-
-    @pl.when(is_diag)
-    def _():
-        own_prompt.wait()
-
-    for n in range(N_ALL):
-        kp[4 * n : 4 * n + 4, :] = pt[n, 0:4, :]
-        vp[4 * n : 4 * n + 4, :] = pt[n, 4:8, :]
-
     def pass_far(k):
         j = lax.rem(k + 4, N_CTX)
 
@@ -324,8 +317,15 @@
             relay_copy(j).start()
 
     loop(0, N_CTX, pass_far)
-    spread_own(*d_way, 5).wait()
     spread_own(*q_way, 6).wait()
+
+    @pl.when(jnp.logical_not(is_diag))
+    def _():
+        column_copy(1).wait_recv()
+
+    for n in range(N_GRP):
+        kp[32 * n : 32 * n + 32, :] = pb[n, 0:32, :]
+        vp[32 * n : 32 * n + 32, :] = pb[n, 32:64, :]
 
     def keys_at(at, count):
         return pl.ds(pl.multiple_of(at, 256), count)
@@ -340,11 +340,11 @@
         return jnp.concatenate([aug[keys_at(at, count), :], kvw[keys_at(at, count), 0:128]], axis=1)
 
     def head_keys(r):
-        first = jnp.concatenate([jnp.zeros((PROMPT_TOKENS, 128), bf16), kp[...].astype(bf16)], axis=1)
+        first = jnp.concatenate([jnp.zeros((PROMPT_TOKENS, 128), bf16), kp[...]], axis=1)
         return jnp.concatenate([first, masked_keys(OWN + r * TQ, TQ)], axis=0)
 
     def head_values(r):
-        return jnp.concatenate([vp[...].astype(bf16), kvw[keys_at(OWN + r * TQ, TQ), 128:256]], axis=0)
+        return jnp.concatenate([vp[...], kvw[keys_at(OWN + r * TQ, TQ), 128:256]], axis=0)
 
     def head_scores(r, qa):
         s = dot_nt(head_keys(r), qa)
@@ -360,23 +360,17 @@
     def forward(k):
         r = ROW_TILES - 1 - k
 
-        @pl.when(has_far & (lax.rem(k, 2) == 0))
-        def _():
-            loop(0, 4, lambda j: relay_copy(4 - 2 * k + j).wait_recv())
-
         for e in range(2):
             j = 2 * r + e
 
             @pl.when(j != c)
             def _():
-                spread_in(*d_way, d_s, d_r, j).wait_recv()
                 spread_in(*q_way, q_s, q_r, j).wait_recv()
 
         at_rows = pl.ds(pl.multiple_of(r * TQ, TQ), TQ)
         for h in range(QH):
             to = pl.ds(pl.multiple_of(r * LANES + h * TQ, TQ), TQ)
             qst[to, :] = qx[at_rows, 128 * h : 128 * h + 128]
-            dost[to, :] = dox[at_rows, 128 * h : 128 * h + 128]
         qa = masked_queries(r)
         low = first_step(r)
 
@@ -390,7 +384,14 @@
             return jnp.maximum(top, jnp.max(s, axis=0, keepdims=True))
 
         top = lax.fori_loop(0, r, lambda t, a: score(OWN + t * TQ, TQ, a), top)
-        top = lax.fori_loop(low, OWN // STEP, lambda t, a: score(t * STEP, STEP, a), top)
+        near_low = jnp.where(has_prev, CHUNK // STEP, OWN // STEP)
+        top = lax.fori_loop(near_low, OWN // STEP, lambda t, a: score(t * STEP, STEP, a), top)
+
+        @pl.when(has_far & (lax.rem(k, 2) == 0))
+        def _():
+            loop(0, 4, lambda j: relay_copy(4 - 2 * k + j).wait_recv())
+
+        top = lax.fori_loop(low, near_low, lambda t, a: score(t * STEP, STEP, a), top)
         top = top * C2
 
         def power(at, total):
@@ -410,6 +411,20 @@
 
         loop(0, r, lambda t: gather(OWN + t * TQ, TQ))
         loop(low, OWN // STEP, lambda t: gather(t * STEP, STEP))
+        for e in range(2):
+            j = 2 * r + e
+
+            @pl.when(j != c)
+            def _():
+                spread_in(*d_way, d_s, d_r, j).wait_recv()
+
+            @pl.when(j == c)
+            def _():
+                spread_own(*d_way, 5).wait()
+
+        for h in range(QH):
+            to = pl.ds(pl.multiple_of(r * LANES + h * TQ, TQ), TQ)
+            dost[to, :] = dox[at_rows, 128 * h : 128 * h + 128]
         o = o_t[...].astype(bf16).astype(f32)
         delta = jnp.sum(o * dost[tile_rows(r), :].astype(f32).T, axis=0, keepdims=True)
         stats[r, 0:1, :] = top + jnp.log(total) * LOG2E
@@ -417,7 +432,6 @@
         o_rows = o.T.astype(bf16)
         for h in range(QH):
             ox[at_rows, 128 * h : 128 * h + 128] = o_rows[TQ * h : TQ * h + TQ, :]
-        dq_all[r] = jnp.zeros((128, LANES), f32)
         send_rows(ox, out, o_s, o_r, r, 7)
 
     def home(src, dst, s, r, width, peer):
@@ -461,12 +475,38 @@
         dkv[here, 0:128] += dot_nn(ds, qst[tile_rows(r), :])
         dkv[here, 128:256] += dot_nn(half, dost[tile_rows(r), :])
 
-    @pl.when(has_far)
-    def _():
-        def far_rows(r):
-            loop(r // 2, CHUNK // STEP, lambda t: backward(r, t * STEP, STEP))
-
-        loop(0, ROW_TILES, far_rows)
+    pkg[...] = jnp.zeros((128, 128), f32)
+    pvg[...] = jnp.zeros((128, 128), f32)
+
+    def prompt_rows(r):
+        half, ds = grads(r, dot_nt(kp[...], qst[tile_rows(r), :]), vp[...])
+        dq_all[r] = dot_tn(kp[...], ds)
+        pkg[...] += dot_nn(ds, qst[tile_rows(r), :])
+        pvg[...] += dot_nn(half, dost[tile_rows(r), :])
+
+    loop(0, ROW_TILES, prompt_rows)
+    for n in range(N_GRP):
+        pgb[n, 0:32, :] = pkg[32 * n : 32 * n + 32, :].astype(bf16)
+        pgb[n, 32:64, :] = pvg[32 * n : 32 * n + 32, :].astype(bf16)
+
+    def to_hub(at):
+        return remote(pgb, pgin.at[at], ga_s.at[0], ga_r.at[at], hub)
+
+    def over_groups(at, k):
+        gg = lax.rem(g + k, N_GRP)
+        return remote(tot.at[gg], bin.at[at], gb_s.at[k], gb_r.at[at], (gg, z, c))
+
+    def to_owner(k):
+        cc = lax.rem(c + k, N_CTX)
+        return remote(ft.at[cc], pfin, gc_s.at[k], gc_r.at[0], (g, z, cc))
+
+    @pl.when(is_diag)
+    def _():
+        pgin[z] = pgb[...]
+
+    @pl.when(jnp.logical_not(is_diag))
+    def _():
+        to_hub(z).start()
 
     def far_copy(j):
         return remote(
@@ -479,19 +519,28 @@
         )
 
     def send_far(j):
-        @pl.when(has_far)
-        def _():
-            far_out[rows(j * BLOCK), :] = dkv[rows(j * BLOCK), :].astype(bf16)
-            far_copy(j).start()
-
-    loop(0, N_CTX, send_far)
-
-    @pl.when(has_prev)
-    def _():
-        def near_rows(r):
-            loop(CHUNK // STEP, OWN // STEP, lambda t: backward(r, t * STEP, STEP))
-
-        loop(0, ROW_TILES, near_rows)
+        far_out[rows(j * BLOCK), :] = dkv[rows(j * BLOCK), :].astype(bf16)
+        far_copy(j).start()
+
+    blocks = STEP // BLOCK
+
+    @pl.when(has_far)
+    def _():
+        def far_keys(t):
+            loop(0, 2 + 2 * t, lambda r: backward(r, t * STEP, STEP))
+            loop(blocks * t, blocks * t + blocks, send_far)
+
+        loop(0, CHUNK // STEP, far_keys)
+
+    @pl.when(is_diag)
+    def _():
+        loop(1, N_ULY, lambda k: to_hub(lax.rem(z + k, N_ULY)).wait_recv())
+        for n in range(N_GRP):
+            part = pgin[0, n].astype(f32)
+            for m in range(1, N_ULY):
+                part = part + pgin[m, n].astype(f32)
+            tot[n] = part
+        bin[g] = tot[g]
 
     def send_near(j):
         mine = dkv[rows(CHUNK + j * BLOCK), :]
@@ -505,29 +554,31 @@
         def _():
             near_out[rows(j * BLOCK), :] = mine.astype(bf16)
 
-        @pl.when(has_prev)
-        def _():
-            near_copy(j).start()
-
-    loop(0, N_CTX, send_near)
-
-    pkg[...] = jnp.zeros((128, 128), f32)
-    pvg[...] = jnp.zeros((128, 128), f32)
+        near_copy(j).start()
+
+    @pl.when(has_prev)
+    def _():
+        def near_keys(t):
+            loop(0, ROW_TILES, lambda r: backward(r, CHUNK + t * STEP, STEP))
+            loop(blocks * t, blocks * t + blocks, send_near)
+
+        loop(0, CHUNK // STEP, near_keys)
+
+    @pl.when(is_diag)
+    def _():
+        loop(1, N_GRP, lambda k: over_groups(g, k).start())
 
     def own_rows(k):
         r = lax.rem(c // 2 + k, ROW_TILES)
         loop(0, r, lambda t: backward(r, OWN + t * TQ, TQ))
-        s = head_scores(r, masked_queries(r))
-        half, ds = grads(r, s, head_values(r))
-        k_head = jnp.concatenate([kp[...].astype(bf16), kvw[keys_at(OWN + r * TQ, TQ), 0:128]], axis=0)
-        back = dq_all[r] + dot_tn(k_head, ds)
-        k_part = dot_nn(ds, qst[tile_rows(r), :])
-        v_part = dot_nn(half, dost[tile_rows(r), :])
-        pkg[...] += k_part[0:PROMPT_TOKENS, :]
-        pvg[...] += v_part[0:PROMPT_TOKENS, :]
         here = keys_at(OWN + r * TQ, TQ)
-        dkv[here, 0:128] += k_part[PROMPT_TOKENS:HEAD_KEYS, :]
-        dkv[here, 128:256] += v_part[PROMPT_TOKENS:HEAD_KEYS, :]
+        s = dot_nt(masked_keys(OWN + r * TQ, TQ), masked_queries(r))
+        key = lax.broadcasted_iota(i32, (TQ, LANES), 0)
+        token = lax.broadcasted_iota(i32, (TQ, LANES), 1) % TQ
+        half, ds = grads(r, jnp.where(key <= token, s, neg_fill), kvw[here, 128:256])
+        back = dq_all[r] + dot_tn(kvw[here, 0:128], ds)
+        dkv[here, 0:128] += dot_nn(ds, qst[tile_rows(r), :])
+        dkv[here, 128:256] += dot_nn(half, dost[tile_rows(r), :])
         tau = start + r * TQ + lax.broadcasted_iota(i32, (1, TQ), 1)
         pos = (PROMPT_TOKENS + tau - begins_of(tau, lens)).astype(f32)
         angle = frequency_of(lax.broadcasted_iota(i32, (64, TQ), 0)) * pos
@@ -543,25 +594,6 @@
 
     loop(0, ROW_TILES, own_rows)
 
-    for n in range(N_ALL):
-        pg[n, 0:4, :] = pkg[4 * n : 4 * n + 4, :]
-        pg[n, 4:8, :] = pvg[4 * n : 4 * n + 4, :]
-
-    def prompt_back(n):
-        return remote(pg.at[n], pin.at[me_back], pg_s.at[n], pg_r.at[me_back], at_row(n))
-
-    def start_back(n):
-        @pl.when(jnp.logical_not(row_is_me(n)))
-        def _():
-            prompt_back(n).start()
-
-    loop(0, N_ALL, start_back)
-    own_back = pltpu.make_async_copy(pg.at[me_in], pin.at[me_back], loc.at[9])
-
-    @pl.when(is_diag)
-    def _():
-        own_back.start()
-
     def finish_block(total, j):
         x = total[:, 0:128]
         cosine_j, sine_j = cosines[rows(j * BLOCK), :], sines[rows(j * BLOCK), :]
@@ -590,23 +622,30 @@
     home_own(own.at[0], dk, 128, 10).start()
     home_own(own.at[1], dv, 128, 11).start()
 
-    def finish_prompt(n):
-        @pl.when(jnp.logical_not(column_is_me(n)))
-        def _():
-            prompt_copy(n).wait_send()
-            remote(pg.at[n], pin.at[n], pg_s.at[n], pg_r.at[n], at_column(n)).wait_recv()
-
-        @pl.when(jnp.logical_not(row_is_me(n)))
-        def _():
-            prompt_back(n).wait_send()
-
-    loop(0, N_ALL, finish_prompt)
-
-    @pl.when(is_diag)
-    def _():
-        own_back.wait()
-
-    total = jnp.sum(pin[...], axis=0)
+    @pl.when(is_diag)
+    def _():
+        loop(1, N_GRP, lambda k: over_groups(lax.rem(g + k, N_GRP), k).wait_recv())
+        whole = bin[0] + bin[1] + bin[2] + bin[3]
+        for n in range(N_CTX):
+            ft[n, 0:4, :] = whole[4 * n : 4 * n + 4, :]
+            ft[n, 4:8, :] = whole[32 + 4 * n : 36 + 4 * n, :]
+        loop(1, N_CTX, lambda k: to_owner(k).start())
+        pfin[...] = ft[c]
+
+    @pl.when(is_diag)
+    def _():
+        loop(1, N_GRP, lambda k: group_copy(g, k).wait_send())
+        loop(1, N_ULY, lambda k: column_copy(k).wait_send())
+        loop(1, N_GRP, lambda k: over_groups(g, k).wait_send())
+        loop(1, N_CTX, lambda k: to_owner(k).wait_send())
+
+    @pl.when(jnp.logical_not(is_diag))
+    def _():
+        tile_copy(c).wait_send()
+        to_hub(z).wait_send()
+        to_owner(1).wait_recv()
+
+    total = pfin[...]
     dpk[...] = total[0:4, :].astype(bf16)
     dpv[...] = total[4:8, :].astype(bf16)
 
@@ -681,16 +720,20 @@
     results = pl.pallas_call(
         step_kernel,
         out_shape=shapes,
-        in_specs=[spec(HBM)] * 4 + [spec(SMEM), spec(VMEM), spec(VMEM)],
+        in_specs=[spec(HBM)] * 4 + [spec(SMEM), spec(HBM), spec(HBM)],
         out_specs=(spec(VMEM),) * 6,
         scratch_shapes=[
             VMEM((BLOCK, 4096), bf16),
             VMEM((BLOCK, 1024), bf16),
             VMEM((BLOCK, 1024), bf16),
+            VMEM((4, 128), bf16),
+            VMEM((4, 128), bf16),
             VMEM((BLOCK, 4096), bf16),
             VMEM((BLOCK, 2048), bf16),
             VMEM((8, 128), f32),
-            VMEM((N_ALL, 8, 128), f32),
+            VMEM((N_CTX, 8, 128), f32),
+            VMEM((64, 128), f32),
+            VMEM((N_GRP, 64, 128), bf16),
             VMEM((CHUNK, 512), bf16),
             VMEM((CHUNK, 512), bf16),
             VMEM((WIN, 256), bf16),
@@ -698,8 +741,8 @@
             VMEM((ROW_TILES * LANES, 128), bf16),
             VMEM((ROW_TILES * LANES, 128), bf16),
             VMEM((ROW_TILES * LANES, 128), bf16),
-            VMEM((128, 128), f32),
-            VMEM((128, 128), f32),
+            VMEM((128, 128), bf16),
+            VMEM((128, 128), bf16),
             VMEM((HEAD_AT + HEAD_KEYS, LANES), f32),
             VMEM((128, LANES), f32),
             VMEM((ROW_TILES, 128, LANES), f32),
@@ -707,16 +750,20 @@
             VMEM((WIN, 256), f32),
             VMEM((128, 128), f32),
             VMEM((128, 128), f32),
-            VMEM((N_ALL, 8, 128), f32),
-            VMEM((N_ALL, 8, 128), f32),
+            VMEM((N_GRP, 64, 128), bf16),
+            VMEM((N_ULY, N_GRP, 64, 128), bf16),
+            VMEM((N_GRP, 64, 128), f32),
+            VMEM((N_GRP, 64, 128), f32),
+            VMEM((N_CTX, 8, 128), f32),
+            VMEM((8, 128), f32),
             VMEM((CHUNK, 512), bf16),
             VMEM((CHUNK, 512), bf16),
         ]
         + [VMEM((CHUNK, 256), bf16)] * 4
         + [VMEM((2, CHUNK, 128), bf16), VMEM((CHUNK, 128), f32), VMEM((CHUNK, 128), f32)]
         + [DMA((8,))] * 22
-        + [DMA((N_ALL,))] * 4
-        + [DMA((12,))],
+        + [DMA((8,))] * 12
+        + [DMA((14,))],
         compiler_params=pltpu.CompilerParams(
             collective_id=0, has_side_effects=True, vmem_limit_bytes=56 << 20
         ),

time: 128 us -> 123 us (0.961); the launches traced: 126 us -> 123 us
  Pallas kernels: 126 us -> 122 us
    pallas_call x1, Pallas kernels: 122 us -> 119 us  [local(): pl.pallas_call(step_kernel, out_shape=shapes, in_specs=[spec(HBM)] * 4 +...]
where the time goes in v3:
time: 123 us
  Pallas kernels  122 us (99%)
    pallas_call x1, Pallas kernels, local(): pl.pallas_call(step_kernel, out_shape=shapes, in_specs=[spec(HBM)] * 4 +...  119 us
    pallas_call x1, Pallas kernels, local(): pl.pallas_call(place, out_shape=shapes, in_specs=[spec(VMEM)] * 6, out_sp...  3.2 us

profile of v3, /device:TPU:64, one launch (start us, length us, event | category | flops | bytes accessed | tf_op | source)
XLA Modules:
  0.0 123.0 jit_solution(8060281750136182509)
XLA Ops:
  0.6 119.2 %grpo_step.1 = (bf16[128,4096]{1,0:T(8,128)(2,1)}, bf16[128,4096]{1,0:T(8,128)(2,1)}, bf16[128,1024]{1,0:T(8,128)(2,1)}, bf16[128,1024]{1,0:T(8,128)(2,1)}, bf16...) custom-call(bf16[128,4096]{1,0:T(8,128)(2,1)} %q_hbm.1, bf16[128,4096]{1,0:T(8,128)(2,1)} %do_hbm.1, bf16[128,1024]{1,0:T(8,128)(2,1)} %k_hbm.1, ...), custom_call_target="tpu_custom_call" | custom-call | tf_op jit(solution)/shard_map/grpo_step/pallas_call | solution.py:720
  119.8 3.2 %place.1 = (bf16[128,4096]{1,0:T(8,128)(2,1)}, bf16[128,4096]{1,0:T(8,128)(2,1)}, bf16[128,1024]{1,0:T(8,128)(2,1)}, bf16[128,1024]{1,0:T(8,128)(2,1)}, bf16[4,128]{1,0:T(4,128)(2,1)}, /*index=5*/bf16[4,128]{1,0:T(4,128)(2,1)}) custom-call(bf16[128,4096]{1,0:T(8,128)(2,1)} %get-tuple-element.12.refs_0_, bf16[128,4096]{1,0:T(8,128)(2,1)} %get-tuple-element.13.refs_1_, ...), custom_call_target="tpu_custom_call" | custom-call | tf_op jit(solution)/shard_map/place/pallas_call | solution.py:772

commit v4 on v3

--- a/solution.py
+++ b/solution.py
@@ -385,7 +385,8 @@
 
         top = lax.fori_loop(0, r, lambda t, a: score(OWN + t * TQ, TQ, a), top)
         near_low = jnp.where(has_prev, CHUNK // STEP, OWN // STEP)
-        top = lax.fori_loop(near_low, OWN // STEP, lambda t, a: score(t * STEP, STEP, a), top)
+        near_from = jnp.where(has_prev, 1, OWN // CHUNK)
+        top = lax.fori_loop(near_from, OWN // CHUNK, lambda t, a: score(t * CHUNK, CHUNK, a), top)
 
         @pl.when(has_far & (lax.rem(k, 2) == 0))
         def _():
@@ -401,7 +402,8 @@
 
         total = power(head_at, jnp.zeros((1, LANES), f32))
         total = lax.fori_loop(0, r, lambda t, a: power(keys_at(OWN + t * TQ, TQ), a), total)
-        total = lax.fori_loop(low, OWN // STEP, lambda t, a: power(keys_at(t * STEP, STEP), a), total)
+        total = lax.fori_loop(low, near_low, lambda t, a: power(keys_at(t * STEP, STEP), a), total)
+        total = lax.fori_loop(near_from, OWN // CHUNK, lambda t, a: power(keys_at(t * CHUNK, CHUNK), a), total)
         inverse = 1.0 / total
         o_t[...] = dot_tn(head_values(r), (s_all[head_at, :] * inverse).astype(bf16))
 
@@ -410,7 +412,8 @@
             o_t[...] += dot_tn(kvw[keys_at(at, count), 128:256], half)
 
         loop(0, r, lambda t: gather(OWN + t * TQ, TQ))
-        loop(low, OWN // STEP, lambda t: gather(t * STEP, STEP))
+        loop(low, near_low, lambda t: gather(t * STEP, STEP))
+        loop(near_from, OWN // CHUNK, lambda t: gather(t * CHUNK, CHUNK))
         for e in range(2):
             j = 2 * r + e
 
@@ -601,7 +604,7 @@
         own[1, rows(j * BLOCK), :] = total[:, 128:256].astype(bf16)
 
     def send_own(k):
-        j = lax.rem(c + k, N_CTX)
+        j = 4 * (k // 4) + lax.rem(c + k, 4)
         mine = dkv[rows(OWN + j * BLOCK), :]
 
         @pl.when(has_next)
@@ -613,12 +616,12 @@
         def _():
             finish_block(mine, j)
 
-        @pl.when(k < N_CTX)
+        @pl.when(j != c)
         def _():
             home(own.at[0], dk, k_s, k_r, 128, j).start()
             home(own.at[1], dv, v_s, v_r, 128, j).start()
 
-    loop(1, N_CTX + 1, send_own)
+    loop(0, N_CTX, send_own)
     home_own(own.at[0], dk, 128, 10).start()
     home_own(own.at[1], dv, 128, 11).start()
 

time: 123 us -> 122 us (level); the launches traced: 123 us -> 120 us
  Pallas kernels: 122 us -> 119 us
    pallas_call x1, Pallas kernels: 119 us -> 116 us  [local(): pl.pallas_call(step_kernel, out_shape=shapes, in_specs=[spec(HBM)] * 4 +...]
where the time goes in v4:
time: 122 us; the launch traced here: 120 us
  Pallas kernels  119 us (98%)
    pallas_call x1, Pallas kernels, local(): pl.pallas_call(step_kernel, out_shape=shapes, in_specs=[spec(HBM)] * 4 +...  116 us
    pallas_call x1, Pallas kernels, local(): pl.pallas_call(place, out_shape=shapes, in_specs=[spec(VMEM)] * 6, out_sp...  3.2 us

profile of v4, /device:TPU:64, one launch (start us, length us, event | category | flops | bytes accessed | tf_op | source)
XLA Modules:
  0.0 119.8 jit_solution(9322896773505127998)
XLA Ops:
  0.6 115.9 %grpo_step.1 = (bf16[128,4096]{1,0:T(8,128)(2,1)}, bf16[128,4096]{1,0:T(8,128)(2,1)}, bf16[128,1024]{1,0:T(8,128)(2,1)}, bf16[128,1024]{1,0:T(8,128)(2,1)}, bf16...) custom-call(bf16[128,4096]{1,0:T(8,128)(2,1)} %q_hbm.1, bf16[128,4096]{1,0:T(8,128)(2,1)} %do_hbm.1, bf16[128,1024]{1,0:T(8,128)(2,1)} %k_hbm.1, ...), custom_call_target="tpu_custom_call" | custom-call | tf_op jit(solution)/shard_map/grpo_step/pallas_call | solution.py:723
  116.6 3.2 %place.1 = (bf16[128,4096]{1,0:T(8,128)(2,1)}, bf16[128,4096]{1,0:T(8,128)(2,1)}, bf16[128,1024]{1,0:T(8,128)(2,1)}, bf16[128,1024]{1,0:T(8,128)(2,1)}, bf16[4,128]{1,0:T(4,128)(2,1)}, /*index=5*/bf16[4,128]{1,0:T(4,128)(2,1)}) custom-call(bf16[128,4096]{1,0:T(8,128)(2,1)} %get-tuple-element.12.refs_0_, bf16[128,4096]{1,0:T(8,128)(2,1)} %get-tuple-element.13.refs_1_, ...), custom_call_target="tpu_custom_call" | custom-call | tf_op jit(solution)/shard_map/place/pallas_call | solution.py:775

commit v5 on v4

--- a/solution.py
+++ b/solution.py
@@ -319,14 +319,6 @@
     loop(0, N_CTX, pass_far)
     spread_own(*q_way, 6).wait()
 
-    @pl.when(jnp.logical_not(is_diag))
-    def _():
-        column_copy(1).wait_recv()
-
-    for n in range(N_GRP):
-        kp[32 * n : 32 * n + 32, :] = pb[n, 0:32, :]
-        vp[32 * n : 32 * n + 32, :] = pb[n, 32:64, :]
-
     def keys_at(at, count):
         return pl.ds(pl.multiple_of(at, 256), count)
 
@@ -356,6 +348,15 @@
 
     def first_step(r):
         return jnp.where(has_far, r // 2, jnp.where(has_prev, CHUNK // STEP, OWN // STEP))
+
+    def take_prompt():
+        @pl.when(jnp.logical_not(is_diag))
+        def _():
+            column_copy(1).wait_recv()
+
+        for n in range(N_GRP):
+            kp[32 * n : 32 * n + 32, :] = pb[n, 0:32, :]
+            vp[32 * n : 32 * n + 32, :] = pb[n, 32:64, :]
 
     def forward(k):
         r = ROW_TILES - 1 - k
@@ -374,9 +375,7 @@
         qa = masked_queries(r)
         low = first_step(r)
 
-        s = head_scores(r, qa)
-        s_all[head_at, :] = s
-        top = jnp.max(s, axis=0, keepdims=True)
+        top = jnp.full((1, LANES), neg_fill, f32)
 
         def score(at, count, top):
             s = dot_nt(masked_keys(at, count), qa)
@@ -393,6 +392,14 @@
             loop(0, 4, lambda j: relay_copy(4 - 2 * k + j).wait_recv())
 
         top = lax.fori_loop(low, near_low, lambda t, a: score(t * STEP, STEP, a), top)
+
+        @pl.when(k == 0)
+        def _():
+            take_prompt()
+
+        s = head_scores(r, qa)
+        s_all[head_at, :] = s
+        top = jnp.maximum(top, jnp.max(s, axis=0, keepdims=True))
         top = top * C2
 
         def power(at, total):

time: 122 us -> 121 us (level)
  no operation moved by 1% of the time
where the time goes in v5:
time: 121 us; the launch traced here: 119 us
  Pallas kernels  118 us (98%)
    pallas_call x1, Pallas kernels, local(): pl.pallas_call(step_kernel, out_shape=shapes, in_specs=[spec(HBM)] * 4 +...  115 us
    pallas_call x1, Pallas kernels, local(): pl.pallas_call(place, out_shape=shapes, in_specs=[spec(VMEM)] * 6, out_sp...  3.2 us

profile of v5, /device:TPU:64, one launch (start us, length us, event | category | flops | bytes accessed | tf_op | source)
XLA Modules:
  0.0 118.8 jit_solution(2380301120775720211)
XLA Ops:
  0.6 115.0 %grpo_step.1 = (bf16[128,4096]{1,0:T(8,128)(2,1)}, bf16[128,4096]{1,0:T(8,128)(2,1)}, bf16[128,1024]{1,0:T(8,128)(2,1)}, bf16[128,1024]{1,0:T(8,128)(2,1)}, bf16...) custom-call(bf16[128,4096]{1,0:T(8,128)(2,1)} %q_hbm.1, bf16[128,4096]{1,0:T(8,128)(2,1)} %do_hbm.1, bf16[128,1024]{1,0:T(8,128)(2,1)} %k_hbm.1, ...), custom_call_target="tpu_custom_call" | custom-call | tf_op jit(solution)/shard_map/grpo_step/pallas_call | solution.py:730
  115.6 3.2 %place.1 = (bf16[128,4096]{1,0:T(8,128)(2,1)}, bf16[128,4096]{1,0:T(8,128)(2,1)}, bf16[128,1024]{1,0:T(8,128)(2,1)}, bf16[128,1024]{1,0:T(8,128)(2,1)}, bf16[4,128]{1,0:T(4,128)(2,1)}, /*index=5*/bf16[4,128]{1,0:T(4,128)(2,1)}) custom-call(bf16[128,4096]{1,0:T(8,128)(2,1)} %get-tuple-element.12.refs_0_, bf16[128,4096]{1,0:T(8,128)(2,1)} %get-tuple-element.13.refs_1_, ...), custom_call_target="tpu_custom_call" | custom-call | tf_op jit(solution)/shard_map/place/pallas_call | solution.py:782
